TPU v7x, 32 devices: a whole 2x2x4 slice. The times are simulated.
32 devices in a mesh: fsdp: 2 (over y), tensor: 8 (over z, x), ctx: 2 (over core).
Axes of the slice: x: 2, y: 2, z: 4, core: 2. Of those that a mesh axis runs over, the one named last changes fastest.
Arguments:
- hidden_in: bfloat16 [16, 2048, 1024], P('fsdp', ('tensor', 'ctx')), may hold values from -6 to 6
- segment_ids: int32 [16, 2048], P('fsdp'), may hold values from 0 to 3, never falling along the last dimension, each value on 1 to 1024 neighbouring positions
- norm_gains: bfloat16 [2, 1024], replicated, may hold values from 0.5 to 1.5
- norm_biases: bfloat16 [2, 1024], replicated, may hold values from -1.75 to 1.75
- qkv_weight: bfloat16 [1024, 16, 192], P(('fsdp', 'ctx'), 'tensor'), may hold values from -0.1875 to 0.1875
- qkv_bias: bfloat16 [16, 192], P('tensor'), may hold values from -1.75 to 1.75
- dense_weight: bfloat16 [16, 64, 1024], P('tensor', None, ('fsdp', 'ctx')), may hold values from -2 to 2
- fc_in_weight: bfloat16 [1024, 4096], P(('fsdp', 'ctx'), 'tensor'), may hold values from -0.1875 to 0.1875
- fc_in_bias: bfloat16 [4096], P('tensor'), may hold values from -3 to 3
- fc_out_weight: bfloat16 [4096, 1024], P('tensor', ('fsdp', 'ctx')), may hold values from -0.09375 to 0.09375
- out_biases: bfloat16 [2, 1024], replicated, may hold values from -1.75 to 1.75
- out_grad: bfloat16 [16, 2048, 1024], P('fsdp', ('tensor', 'ctx')), may hold values from -6 to 6
Outputs:
- hidden_out: bfloat16 [16, 2048, 1024], P('fsdp', ('tensor', 'ctx'))
- input_grad: bfloat16 [16, 2048, 1024], P('fsdp', ('tensor', 'ctx'))
- gain_grads: float32 [2, 1024], replicated
- norm_bias_grads: float32 [2, 1024], replicated
- qkv_weight_grad: float32 [1024, 16, 192], P(('fsdp', 'ctx'), 'tensor')
- qkv_bias_grad: float32 [16, 192], P('tensor')
- dense_weight_grad: float32 [16, 64, 1024], P('tensor', None, ('fsdp', 'ctx'))
- fc_in_weight_grad: float32 [1024, 4096], P(('fsdp', 'ctx'), 'tensor')
- fc_in_bias_grad: float32 [4096], P('tensor')
- fc_out_weight_grad: float32 [4096, 1024], P('tensor', ('fsdp', 'ctx'))
- out_bias_grads: float32 [2, 1024], replicated
Inputs may be any that keep to these rules, and one draw needn't show every extreme that they name: `segment_ids`: along each sequence the numbers never fall; each of 0 to 3 covers 1 to 1024 positions, and one covers exactly 1024.
All inputs are finite; a program needn't handle non-finite values.
Results may differ from a plain program's by a relative error of at most 0.011.
Values may be sent and summed in bfloat16 or wider, within the bound.
No kernel may reach another device: no remote copies, remote signals or barrier semaphores. Data moves between devices by JAX's collectives and lax.ppermute only.
A program may use at most 256 MiB of HBM per device.

v0:
```python
import jax
import jax.numpy as jnp
from jax import lax
from jax.sharding import PartitionSpec as P

HD = 64
ROT = 16
MICRO = 2


epsilon = 1e-05


def partner(x, axis, bit):
    return lax.ppermute(x, axis, [(i, i ^ 1 << bit) for i in range(lax.axis_size(axis))])


def layer_stats(values):
    center = values - jnp.mean(values, axis=-1, keepdims=True)
    inverse = lax.rsqrt(jnp.mean(center * center, axis=-1, keepdims=True) + epsilon)
    return (center * inverse, inverse)


def norm_back(upstream, normed, inverse, gain_row):
    scaled = upstream * gain_row
    return inverse * (
        scaled
        - jnp.mean(scaled, axis=-1, keepdims=True)
        - normed * jnp.mean(scaled * normed, axis=-1, keepdims=True)
    )


def rotary_tables(segments, rotary):
    places = lax.broadcasted_iota(jnp.int32, segments.shape, 1)
    change = jnp.concatenate(
        [jnp.ones_like(segments[:, :1]), (segments[:, 1:] != segments[:, :-1]).astype(jnp.int32)],
        axis=1,
    )
    starts = lax.cummax(places * change, axis=1)
    relative = (places - starts).astype(jnp.float32)
    freqs = 10000.0 ** (-jnp.arange(0, rotary, 2, dtype=jnp.float32) / rotary)
    angle = relative[..., None] * freqs
    angle = jnp.concatenate([angle, angle], axis=-1)
    return (jnp.cos(angle), jnp.sin(angle))


def rotate(values, cosine, sine_part, rotary):
    half_size = rotary // 2
    head_part = values[..., :rotary]
    turned = jnp.concatenate([-head_part[..., half_size:], head_part[..., :half_size]], axis=-1)
    return jnp.concatenate([head_part * cosine + turned * sine_part, values[..., rotary:]], axis=-1)


def rotate_back(upstream, cosine, sine_part, rotary):
    half_size = rotary // 2
    head_part = upstream[..., :rotary]
    weighted = head_part * sine_part
    turned = jnp.concatenate([weighted[..., half_size:], -weighted[..., :half_size]], axis=-1)
    return jnp.concatenate([head_part * cosine + turned, upstream[..., rotary:]], axis=-1)


def gelu_slope(preact):
    normal_cdf = 0.5 * (1.0 + lax.erf(preact * 0.7071067811865476))
    return normal_cdf + preact * jnp.exp(-0.5 * preact * preact) * 0.3989422804014327


def allowed_mask(seg_query, seg_key, pos_query, pos_key):
    return (seg_query[:, None] == seg_key[None, :]) & (pos_key[None, :] <= pos_query[:, None])


def masked_scores(query_seq, key_seq, allowed, score_scale):
    raw_scores = (
        jnp.einsum("qhe,khe->hqk", query_seq, key_seq, preferred_element_type=jnp.float32)
        * score_scale
    )
    return jnp.where(allowed[None], raw_scores, -1e30)


def body(
    hidden_in,
    segment_ids,
    norm_gains,
    norm_biases,
    qkv_weight,
    qkv_bias,
    dense_weight,
    fc_in_weight,
    fc_in_bias,
    fc_out_weight,
    out_biases,
    out_grad,
):
    tensor_count = lax.axis_size("tensor")
    ctx_index = lax.axis_index("ctx")
    local_seqs, span_len, feature_count = hidden_in.shape
    gathered_len = span_len * tensor_count
    head_count = qkv_bias.shape[0]
    unit_count = fc_in_bias.shape[0]
    seq_block = local_seqs // MICRO
    token_total = seq_block * gathered_len
    score_scale = HD ** (-0.5)
    gain_rows = norm_gains.astype(jnp.float32)
    shift_rows = norm_biases.astype(jnp.float32)
    bias_rows = out_biases.astype(jnp.float32)
    qkv_shift = qkv_bias.astype(jnp.float32)
    unit_shift = fc_in_bias.astype(jnp.float32)
    cosine_all, sine_all = rotary_tables(segment_ids, ROT)
    places = lax.broadcasted_iota(jnp.int32, segment_ids.shape, 1)

    def pick_ctx(table_in, which_ctx):
        shaped = table_in.reshape(
            (table_in.shape[0], tensor_count, 2, span_len) + table_in.shape[2:]
        )
        chosen = lax.dynamic_index_in_dim(shaped, which_ctx, 2, keepdims=False)
        return chosen.reshape((table_in.shape[0], gathered_len) + table_in.shape[2:])

    other_index = 1 - ctx_index
    seg_own = pick_ctx(segment_ids, ctx_index)
    seg_keys = jnp.concatenate([seg_own, pick_ctx(segment_ids, other_index)], axis=1)
    pos_own = pick_ctx(places, ctx_index)
    pos_keys = jnp.concatenate([pos_own, pick_ctx(places, other_index)], axis=1)
    cos_own = pick_ctx(cosine_all, ctx_index)[:, :, None, :]
    sin_own = pick_ctx(sine_all, ctx_index)[:, :, None, :]

    def fetch_weights():
        return (
            lax.all_gather(qkv_weight, ("fsdp", "ctx"), axis=0, tiled=True),
            lax.all_gather(dense_weight, ("fsdp", "ctx"), axis=2, tiled=True),
            lax.all_gather(fc_in_weight, ("fsdp", "ctx"), axis=0, tiled=True),
            lax.all_gather(fc_out_weight, ("fsdp", "ctx"), axis=1, tiled=True),
        )

    acc_qkv = jnp.zeros((feature_count, head_count, 3 * HD), jnp.float32)
    acc_dense = jnp.zeros((head_count, HD, feature_count), jnp.float32)
    acc_in = jnp.zeros((feature_count, unit_count), jnp.float32)
    acc_out = jnp.zeros((unit_count, feature_count), jnp.float32)
    acc_qkv_shift = jnp.zeros((head_count, 3 * HD), jnp.float32)
    acc_unit = jnp.zeros((unit_count,), jnp.float32)
    acc_gain = jnp.zeros((2, feature_count), jnp.float32)
    acc_shift = jnp.zeros((2, feature_count), jnp.float32)
    acc_bias_out = jnp.zeros((feature_count,), jnp.float32)
    outputs = []
    grads_in = []
    for micro_step in range(MICRO):
        start_seq = micro_step * seq_block
        rows_x = hidden_in[start_seq : start_seq + seq_block]
        rows_dy = out_grad[start_seq : start_seq + seq_block]
        weights = fetch_weights()
        w_qkv, w_dense, w_in, w_out = weights
        normed, inverse = layer_stats(rows_x.astype(jnp.float32))
        first_part = (normed * gain_rows[0] + shift_rows[0]).astype(jnp.bfloat16)
        second_part = (normed * gain_rows[1] + shift_rows[1]).astype(jnp.bfloat16)
        first_norm = lax.all_gather(first_part, "tensor", axis=1, tiled=True)
        second_norm = lax.all_gather(second_part, "tensor", axis=1, tiled=True)
        kept_rows = rows_x
        first_flat = first_norm.reshape(token_total, feature_count)
        second_flat = second_norm.reshape(token_total, feature_count)
        qkv_all = jnp.dot(
            first_flat,
            w_qkv.reshape(feature_count, head_count * 3 * HD),
            preferred_element_type=jnp.float32,
        )
        qkv_all = qkv_all.reshape(seq_block, gathered_len, head_count, 3 * HD) + qkv_shift
        cosine = cos_own[start_seq : start_seq + seq_block]
        sine_part = sin_own[start_seq : start_seq + seq_block]
        queries = rotate(qkv_all[..., :HD], cosine, sine_part, ROT).astype(jnp.bfloat16)
        key_part = rotate(qkv_all[..., HD : 2 * HD], cosine, sine_part, ROT).astype(jnp.bfloat16)
        own_kv = jnp.concatenate([key_part, qkv_all[..., 2 * HD :].astype(jnp.bfloat16)], axis=-1)
        far_kv = partner(own_kv, "ctx", 0)
        keys_all = jnp.concatenate([own_kv, far_kv], axis=1)

        def attend(block_item):
            query_seq, kv_seq, seg_query, seg_key, pos_query, pos_key = block_item
            scores = masked_scores(
                query_seq,
                kv_seq[..., :HD],
                allowed_mask(seg_query, seg_key, pos_query, pos_key),
                score_scale,
            )
            top_score = jnp.max(scores, axis=-1, keepdims=True)
            exp_values = jnp.exp(scores - top_score)
            row_total = jnp.sum(exp_values, axis=-1, keepdims=True)
            prob_low = (exp_values / row_total).astype(jnp.bfloat16)
            result = jnp.einsum(
                "hqk,khe->qhe", prob_low, kv_seq[..., HD:], preferred_element_type=jnp.float32
            )
            return (result.astype(jnp.bfloat16), (top_score + jnp.log(row_total))[..., 0])

        attended, log_total = lax.map(
            attend,
            (
                queries,
                keys_all,
                seg_own[start_seq : start_seq + seq_block],
                seg_keys[start_seq : start_seq + seq_block],
                pos_own[start_seq : start_seq + seq_block],
                pos_keys[start_seq : start_seq + seq_block],
            ),
        )
        preact = jnp.dot(second_flat, w_in, preferred_element_type=jnp.float32) + unit_shift
        active = jax.nn.gelu(preact, approximate=False).astype(jnp.bfloat16)
        kept = (
            kept_rows,
            first_flat,
            second_flat,
            queries,
            keys_all,
            attended,
            log_total,
            preact,
            active,
        )
        attended, active = (kept[5], kept[8])
        w_qkv, w_dense, w_in, w_out = weights
        flat_att = attended.reshape(token_total, head_count * HD)
        dense_flat = w_dense.reshape(head_count * HD, feature_count)
        partial_value = jnp.dot(flat_att, dense_flat, preferred_element_type=jnp.float32) + jnp.dot(
            active, w_out, preferred_element_type=jnp.float32
        )
        summed = lax.psum_scatter(
            partial_value.reshape(seq_block, gathered_len, feature_count),
            "tensor",
            scatter_dimension=1,
            tiled=True,
        )
        outputs.append(
            (rows_x.astype(jnp.float32) + summed + bias_rows[0] + bias_rows[1]).astype(jnp.bfloat16)
        )
        weights = fetch_weights()
        w_qkv, w_dense, w_in, w_out = weights
        dense_flat = w_dense.reshape(head_count * HD, feature_count)
        (
            kept_rows,
            first_flat,
            second_flat,
            queries,
            keys_all,
            attended,
            log_total,
            preact,
            active,
        ) = kept
        flat_att = attended.reshape(token_total, head_count * HD)
        dy_whole = lax.all_gather(rows_dy, "tensor", axis=1, tiled=True)
        dy_flat = dy_whole.reshape(token_total, feature_count)
        grad_active = jnp.einsum("td,ud->tu", dy_flat, w_out, preferred_element_type=jnp.float32)
        acc_out = acc_out + jnp.einsum(
            "tu,td->ud", active, dy_flat, preferred_element_type=jnp.float32
        )
        grad_pre = (grad_active * gelu_slope(preact)).astype(jnp.bfloat16)
        acc_in = acc_in + jnp.einsum(
            "td,tu->du", second_flat, grad_pre, preferred_element_type=jnp.float32
        )
        acc_unit = acc_unit + jnp.sum(grad_pre.astype(jnp.float32), axis=0)
        grad_second = jnp.einsum("tu,du->td", grad_pre, w_in, preferred_element_type=jnp.float32)
        grad_att = jnp.einsum(
            "td,ed->te", dy_flat, dense_flat, preferred_element_type=jnp.float32
        ).astype(jnp.bfloat16)
        acc_dense = acc_dense + jnp.einsum(
            "te,td->ed", flat_att, dy_flat, preferred_element_type=jnp.float32
        ).reshape(head_count, HD, feature_count)
        grad_att = grad_att.reshape(seq_block, gathered_len, head_count, HD)

        def attend_back(block_item):
            query_seq, kv_seq, log_seq, grad_seq, seg_query, seg_key, pos_query, pos_key = (
                block_item
            )
            scores = masked_scores(
                query_seq,
                kv_seq[..., :HD],
                allowed_mask(seg_query, seg_key, pos_query, pos_key),
                score_scale,
            )
            prob_full = jnp.exp(scores - log_seq[..., None])
            grad_prob = jnp.einsum(
                "qhe,khe->hqk", grad_seq, kv_seq[..., HD:], preferred_element_type=jnp.float32
            )
            grad_score = (
                prob_full * (grad_prob - jnp.sum(prob_full * grad_prob, axis=-1, keepdims=True))
            ).astype(jnp.bfloat16)
            grad_query = (
                jnp.einsum(
                    "hqk,khe->qhe", grad_score, kv_seq[..., :HD], preferred_element_type=jnp.float32
                )
                * score_scale
            )
            grad_key = (
                jnp.einsum(
                    "hqk,qhe->khe", grad_score, query_seq, preferred_element_type=jnp.float32
                )
                * score_scale
            )
            grad_value = jnp.einsum(
                "hqk,qhe->khe",
                prob_full.astype(jnp.bfloat16),
                grad_seq,
                preferred_element_type=jnp.float32,
            )
            return (grad_query, jnp.concatenate([grad_key, grad_value], axis=-1))

        grad_queries, grad_kv = lax.map(
            attend_back,
            (
                queries,
                keys_all,
                log_total,
                grad_att,
                seg_own[start_seq : start_seq + seq_block],
                seg_keys[start_seq : start_seq + seq_block],
                pos_own[start_seq : start_seq + seq_block],
                pos_keys[start_seq : start_seq + seq_block],
            ),
        )
        far_grad = partner(grad_kv[:, gathered_len:].astype(jnp.bfloat16), "ctx", 0).astype(
            jnp.float32
        )
        own_grad = grad_kv[:, :gathered_len] + far_grad
        cosine = cos_own[start_seq : start_seq + seq_block]
        sine_part = sin_own[start_seq : start_seq + seq_block]
        grad_qkv = jnp.concatenate(
            [
                rotate_back(grad_queries, cosine, sine_part, ROT),
                rotate_back(own_grad[..., :HD], cosine, sine_part, ROT),
                own_grad[..., HD:],
            ],
            axis=-1,
        ).astype(jnp.bfloat16)
        grad_qkv_flat = grad_qkv.reshape(token_total, head_count * 3 * HD)
        acc_qkv = acc_qkv + jnp.einsum(
            "td,te->de", first_flat, grad_qkv_flat, preferred_element_type=jnp.float32
        ).reshape(feature_count, head_count, 3 * HD)
        acc_qkv_shift = acc_qkv_shift + jnp.sum(grad_qkv.astype(jnp.float32), axis=(0, 1))
        grad_first = jnp.einsum(
            "te,de->td",
            grad_qkv_flat,
            w_qkv.reshape(feature_count, head_count * 3 * HD),
            preferred_element_type=jnp.float32,
        )
        grad_first = grad_first.reshape(seq_block, gathered_len, feature_count)
        grad_second = grad_second.reshape(seq_block, gathered_len, feature_count)
        rows_dy_wide = rows_dy.astype(jnp.float32)
        acc_bias_out = acc_bias_out + jnp.sum(rows_dy_wide, axis=(0, 1))
        grad_one, grad_two = (
            lax.psum_scatter(grad_first, "tensor", scatter_dimension=1, tiled=True),
            lax.psum_scatter(grad_second, "tensor", scatter_dimension=1, tiled=True),
        )
        normed, inverse = layer_stats(rows_x.astype(jnp.float32))
        input_rows_grad = (
            rows_dy_wide
            + norm_back(grad_one, normed, inverse, gain_rows[0])
            + norm_back(grad_two, normed, inverse, gain_rows[1])
        )
        acc_gain = acc_gain + jnp.stack(
            [jnp.sum(grad_one * normed, axis=(0, 1)), jnp.sum(grad_two * normed, axis=(0, 1))]
        )
        acc_shift = acc_shift + jnp.stack(
            [jnp.sum(grad_one, axis=(0, 1)), jnp.sum(grad_two, axis=(0, 1))]
        )
        grads_in.append(input_rows_grad.astype(jnp.bfloat16))
    grad_qkv_w, grad_dense_w, grad_in_w, grad_out_w = (
        lax.psum_scatter(
            acc_qkv.astype(jnp.bfloat16), ("fsdp", "ctx"), scatter_dimension=0, tiled=True
        ).astype(jnp.float32),
        lax.psum_scatter(
            acc_dense.astype(jnp.bfloat16), ("fsdp", "ctx"), scatter_dimension=2, tiled=True
        ).astype(jnp.float32),
        lax.psum_scatter(
            acc_in.astype(jnp.bfloat16), ("fsdp", "ctx"), scatter_dimension=0, tiled=True
        ).astype(jnp.float32),
        lax.psum_scatter(
            acc_out.astype(jnp.bfloat16), ("fsdp", "ctx"), scatter_dimension=1, tiled=True
        ).astype(jnp.float32),
    )
    grad_qkv_b, grad_unit_b = lax.psum((acc_qkv_shift, acc_unit), ("fsdp", "ctx"))
    grad_gain, grad_shift, grad_bias = lax.psum(
        (acc_gain, acc_shift, jnp.stack([acc_bias_out, acc_bias_out])), ("fsdp", "tensor", "ctx")
    )
    hidden_out = jnp.concatenate(outputs, axis=0)
    input_grad = jnp.concatenate(grads_in, axis=0)
    return (
        hidden_out,
        input_grad,
        grad_gain,
        grad_shift,
        grad_qkv_w,
        grad_qkv_b,
        grad_dense_w,
        grad_in_w,
        grad_unit_b,
        grad_out_w,
        grad_bias,
    )


def solution(mesh):
    placed = (
        P("fsdp", ("tensor", "ctx"), None),
        P("fsdp", None),
        P(),
        P(),
        P(("fsdp", "ctx"), "tensor", None),
        P("tensor", None),
        P("tensor", None, ("fsdp", "ctx")),
        P(("fsdp", "ctx"), "tensor"),
        P("tensor"),
        P("tensor", ("fsdp", "ctx")),
        P(),
        P("fsdp", ("tensor", "ctx"), None),
    )
    return jax.shard_map(
        body,
        mesh=mesh,
        in_specs=placed,
        out_specs=(
            P("fsdp", ("tensor", "ctx"), None),
            P("fsdp", ("tensor", "ctx"), None),
            P(),
            P(),
            P(("fsdp", "ctx"), "tensor", None),
            P("tensor", None),
            P("tensor", None, ("fsdp", "ctx")),
            P(("fsdp", "ctx"), "tensor"),
            P("tensor"),
            P("tensor", ("fsdp", "ctx")),
            P(),
        ),
        check_vma=False,
    )
```

profile of v0, /device:TPU:0, one launch (start us, length us, event | category | flops | bytes accessed | tf_op | source)
XLA Modules:
  0.0 3361.8 jit_solution(16147375534265305172)
XLA Ops:
  47.6 97.3 %all-gather.9.cloned.1.call-done = bf16[4,1024,1024]{2,1,0:T(8,128)(2,1)} async-done(((bf16[4,128,1024]{2,1,0:T(8,128)(2,1)}), bf16[4,1024,1024]{2,1,0:T(8,128)(2,1)}) %all-gather.9.cloned.1.call-update) | async-done | bytes 8388624 | tf_op jit(solution)/shard_map/all_gather | solution.py:153
  158.1 112.6 %all-gather.17.cloned.1.call-done = bf16[4,1024,1024]{2,1,0:T(8,128)(2,1)} async-done(((bf16[4,128,1024]{2,1,0:T(8,128)(2,1)}), bf16[4,1024,1024]{2,1,0:T(8,128)(2,1)}) %all-gather.17.cloned.1.call-update) | async-done | bytes 8388624 | tf_op jit(solution)/shard_map/all_gather | solution.py:153
  288.2 107.9 %all-gather.21.cloned.1.call-done = bf16[4,1024,1024]{2,1,0:T(8,128)(2,1)} async-done(((bf16[4,128,1024]{2,1,0:T(8,128)(2,1)}), bf16[4,1024,1024]{2,1,0:T(8,128)(2,1)}) %all-gather.21.cloned.1.call-update) | async-done | bytes 8388624 | tf_op jit(solution)/shard_map/all_gather | solution.py:244
  419.2 120.3 %all-gather.19.cloned.1.call-done = bf16[4,1024,1024]{2,1,0:T(8,128)(2,1)} async-done(((bf16[4,128,1024]{2,1,0:T(8,128)(2,1)}), bf16[4,1024,1024]{2,1,0:T(8,128)(2,1)}) %all-gather.19.cloned.1.call-update) | async-done | bytes 8388624 | tf_op jit(solution)/shard_map/all_gather | solution.py:154
  551.0 113.6 %all-gather.11.cloned.1.call-done = bf16[4,1024,1024]{2,1,0:T(8,128)(2,1)} async-done(((bf16[4,128,1024]{2,1,0:T(8,128)(2,1)}), bf16[4,1024,1024]{2,1,0:T(8,128)(2,1)}) %all-gather.11.cloned.1.call-update) | async-done | bytes 8388624 | tf_op jit(solution)/shard_map/all_gather | solution.py:154
  664.6 43.4 %fusion.90 = (bf16[4096,512]{1,0:T(8,128)(2,1)}, bf16[4096,512]{1,0:T(8,128)(2,1)}, f32[4096,512]{1,0:T(8,128)}) fusion(f32[512]{0:T(512)S(1)} %convert_element_type.187, f32[4096,512]{1,0:T(8,128)} %fusion.215, bf16[4096,1024]{1,0:T(8,128)(2,1)} %bitcast.508, bf16[1024,512]{1,0:T(8,128)(2,1)S(1)} %copy-done.67), kind=kOutput, calls=%fused_computation.138 | convolution fusion | flops 4571791360 | bytes 34605056 | tf_op jit(solution)/shard_map/dot_general | solution.py:200
  708.0 81.8 %all-gather.23.cloned.1.call-done = bf16[4,1024,1024]{2,1,0:T(8,128)(2,1)} async-done(((bf16[4,128,1024]{2,1,0:T(8,128)(2,1)}), bf16[4,1024,1024]{2,1,0:T(8,128)(2,1)}) %all-gather.23.cloned.1.call-update) | async-done | bytes 8388624 | tf_op jit(solution)/shard_map/all_gather | solution.py:244
  873.8 79.8 %while.48 = (s32[]{:T(128)}, bf16[4,1024,2,64]{1,3,2,0:T(8,128)(2,1)}, f32[4,2,1024]{2,1,0:T(2,128)S(1)}, bf16[4,2048,2,128]{1,3,2,0:T(8,128)(2,1)}, s32[4,1024]...) while((s32[]{:T(128)}, ...), condition=%wide.region_7.8_spmd, body=%wide.region_4.7_spmd.sunk | while | flops 1130493952 | bytes 62530168 | solution.py:189
  959.6 233.3 %while.50 = (s32[]{:T(128)}, f32[4,1024,2,64]{1,3,2,0:T(8,128)}, f32[4,2048,2,128]{1,3,2,0:T(8,128)}, bf16[4,2048,2,128]{1,3,2,0:T(8,128)(2,1)}, s32[4,1024]{1,0...) while((s32[]{:T(128)}, f32[4,1024,2,64]{1,3,2,0:T(8,128)}, ...), condition=%wide.region_18.19_spmd, body=%wide.region_16.18_spmd.sunk | while | flops 2754476032 | bytes 209063312 | solution.py:301
  986.7 13.0 multiply_convert_fusion.4
  1044.9 13.0 multiply_convert_fusion.4
  1103.1 13.0 multiply_convert_fusion.4
  1161.2 13.0 multiply_convert_fusion.4
  1200.9 80.8 %while.49 = (s32[]{:T(128)}, bf16[4,1024,2,64]{1,3,2,0:T(8,128)(2,1)S(1)}, f32[4,2,1024]{2,1,0:T(2,128)S(1)}, bf16[4,2048,2,128]{1,3,2,0:T(8,128)(2,1)}, s32[4,1...) while((s32[]{:T(128)}, ...), condition=%wide.region_14.15_spmd, body=%wide.region_11.14_spmd.sunk | while | flops 1130493952 | bytes 62530168 | solution.py:189
  1287.7 235.0 %while.51 = (s32[]{:T(128)}, f32[4,1024,2,64]{1,3,2,0:T(8,128)}, f32[4,2048,2,128]{1,3,2,0:T(8,128)}, bf16[4,2048,2,128]{1,3,2,0:T(8,128)(2,1)}, s32[4,1024]{1,0...) while((s32[]{:T(128)}, f32[4,1024,2,64]{1,3,2,0:T(8,128)}, ...), condition=%wide.region_27.28_spmd, body=%wide.region_25.27_spmd.sunk | while | flops 2754476032 | bytes 200674640 | solution.py:301
  1315.4 13.0 multiply_convert_fusion.5
  1373.9 13.0 multiply_convert_fusion.5
  1657.1 221.5 %reduce-scatter.17.cloned.1.call-done = f32[4,128,1024]{2,1,0:T(8,128)} async-done(((f32[4,1024,1024]{2,1,0:T(8,128)}), f32[4,128,1024]{2,1,0:T(8,128)}) %reduce-scatter.17.cloned.1.call-update) | async-done | bytes 2097168 | tf_op jit(solution)/shard_map/reduce_scatter | solution.py:345
  1878.6 285.9 %reduce-scatter.21.cloned.1.call-done = f32[4,128,1024]{2,1,0:T(8,128)} async-done(((f32[4,1024,1024]{2,1,0:T(8,128)}), f32[4,128,1024]{2,1,0:T(8,128)}) %reduce-scatter.21.cloned.1.call-update) | async-done | bytes 2097168 | tf_op jit(solution)/shard_map/reduce_scatter | solution.py:345
  2164.5 285.5 %reduce-scatter.15.cloned.1.call-done = f32[4,128,1024]{2,1,0:T(8,128)} async-done(((f32[4,1024,1024]{2,1,0:T(8,128)}), f32[4,128,1024]{2,1,0:T(8,128)}) %reduce-scatter.15.cloned.1.call-update) | async-done | bytes 2097168 | tf_op jit(solution)/shard_map/reduce_scatter | solution.py:344
  2450.0 285.9 %reduce-scatter.19.cloned.1.call-done = f32[4,128,1024]{2,1,0:T(8,128)} async-done(((f32[4,1024,1024]{2,1,0:T(8,128)}), f32[4,128,1024]{2,1,0:T(8,128)}) %reduce-scatter.19.cloned.1.call-update) | async-done | bytes 2097168 | tf_op jit(solution)/shard_map/reduce_scatter | solution.py:344
  2743.3 278.1 %reduce-scatter.13.cloned.1.call-done = f32[4,128,1024]{2,1,0:T(8,128)} async-done(((f32[4,1024,1024]{2,1,0:T(8,128)}), f32[4,128,1024]{2,1,0:T(8,128)}) %reduce-scatter.13.cloned.1.call-update) | async-done | bytes 2097168 | tf_op jit(solution)/shard_map/reduce_scatter | solution.py:220
  3021.4 285.9 %reduce-scatter.11.cloned.1.call-done = f32[4,128,1024]{2,1,0:T(8,128)} async-done(((f32[4,1024,1024]{2,1,0:T(8,128)}), f32[4,128,1024]{2,1,0:T(8,128)}) %reduce-scatter.11.cloned.1.call-update) | async-done | bytes 2097168 | tf_op jit(solution)/shard_map/reduce_scatter | solution.py:220
  3315.0 39.5 %all-reduce.1 = (f32[2,1024]{1,0:T(2,128)}, f32[2,1024]{1,0:T(2,128)}, f32[2,1024]{1,0:T(2,128)}) all-reduce(f32[2,1024]{1,0:T(2,128)S(1)} %maximum_add_fusion.4, f32[2,1024]{1,0:T(2,128)S(1)} %maximum_add_fusion.5, f32[2,1024]{1,0:T(2,128)S(1)} %pad_maximum_fusion.8), channel_id=1, replica_groups=mesh['fsdp'=2,'tensor'=8,'ctx'=2] {'fsdp','tensor','ctx'}, use_global_device_ids=true, to_apply=%region_38.39 | all-reduce | flops 6144 | bytes 49152 | tf_op jit(solution)/shard_map/psum | solution.py:375
  (630 shorter events, 906.3 us)
Async XLA Ops:
  7.2 137.7 %all-gather.9.cloned.1.call-start = ((), (), s32[]{:S(2)}) async-start(), calls=%async_computation.10 | async-start | bytes 9437184 | tf_op jit(solution)/shard_map/all_gather | solution.py:153
  17.1 253.7 %all-gather.17.cloned.1.call-start = ((), (), s32[]{:S(2)}) async-start(), calls=%async_computation.15 | async-start | bytes 9437184 | tf_op jit(solution)/shard_map/all_gather | solution.py:153
  17.9 378.2 %all-gather.21.cloned.1.call-start = ((), (), s32[]{:S(2)}) async-start(), calls=%async_computation.18 | async-start | bytes 9437184 | tf_op jit(solution)/shard_map/all_gather | solution.py:244
  19.6 399.6 %all-gather.13.cloned.1.call-start = ((), (), s32[]{:S(2)}) async-start(), calls=%async_computation.12 | async-start | bytes 1310720 | tf_op jit(solution)/shard_map/all_gather | solution.py:129
  20.2 519.3 %all-gather.19.cloned.1.call-start = ((), (), s32[]{:S(2)}) async-start(), calls=%async_computation.16 | async-start | bytes 9437184 | tf_op jit(solution)/shard_map/all_gather | solution.py:154
  20.8 643.8 %all-gather.11.cloned.1.call-start = ((), (), s32[]{:S(2)}) async-start(), calls=%async_computation.11 | async-start | bytes 9437184 | tf_op jit(solution)/shard_map/all_gather | solution.py:154
  21.3 768.5 %all-gather.23.cloned.1.call-start = ((), (), s32[]{:S(2)}) async-start(), calls=%async_computation.21 | async-start | bytes 9437184 | tf_op jit(solution)/shard_map/all_gather | solution.py:244
  22.1 784.3 %all-gather.15.cloned.1.call-start = ((), (), s32[]{:S(2)}) async-start(), calls=%async_computation.13 | async-start | bytes 1310720 | tf_op jit(solution)/shard_map/all_gather | solution.py:130
  22.9 1620.6 %reduce-scatter.27.cloned.1.call-start = ((), (), s32[]{:S(2)}) async-start(), calls=%async_computation.26 | async-start | bytes 1310720 | tf_op jit(solution)/shard_map/reduce_scatter | solution.py:367
  288.1 580.4 %collective-permute-start = (bf16[4,1024,2,128]{1,3,2,0:T(8,128)(2,1)}, bf16[4,1024,2,128]{1,3,2,0:T(8,128)(2,1)}, u32[]{:S(2)}, u32[]{:S(2)}) collective-permute-start(bf16[4,1024,2,128]{1,3,2,0:T(8,128)(2,1)} %pad_maximum_fusion.2), channel_id=1, source_target_pairs={{0,1},{1,0},{2,3},{3,2},{4,5},{5,4},{6,7},{7,6},{8,9},{9,8},{10,11... | collective-permute-start | bytes 6291464 | tf_op jit(solution)/shard_map/ppermute | solution.py:15
  419.1 777.9 %collective-permute-start.1 = (bf16[4,1024,2,128]{1,3,2,0:T(8,128)(2,1)}, bf16[4,1024,2,128]{1,3,2,0:T(8,128)(2,1)}, u32[]{:S(2)}, u32[]{:S(2)}) collective-permute-start(bf16[4,1024,2,128]{1,3,2,0:T(8,128)(2,1)} %pad_maximum_fusion.3), channel_id=1, source_target_pairs={{0,1},{1,0},{2,3},{3,2},{4,5},{5,4},{6,7},{7,6},{8,9},{9,8},{10,11... | collective-permute-start | bytes 6291464 | tf_op jit(solution)/shard_map/ppermute | solution.py:15
  847.9 797.4 %reduce-scatter.29.cloned.1.call-start = ((), (), s32[]{:S(2)}) async-start(), calls=%async_computation.27 | async-start | bytes 1310720 | tf_op jit(solution)/shard_map/reduce_scatter | solution.py:370
  865.0 782.1 %reduce-scatter.25.cloned.1.call-start = ((), (), s32[]{:S(2)}) async-start(), calls=%async_computation.25 | async-start | bytes 327680 | tf_op jit(solution)/shard_map/reduce_scatter | solution.py:364
  1196.8 342.6 %collective-permute-start.2 = (bf16[4,1024,2,128]{1,3,2,0:T(8,128)(2,1)}, bf16[4,1024,2,128]{1,3,2,0:T(8,128)(2,1)}, u32[]{:S(2)}, u32[]{:S(2)}) collective-permute-start(bf16[4,1024,2,128]{1,3,2,0:T(8,128)(2,1)} %slice.515), channel_id=1, source_target_pairs={{0,1},{1,0},{2,3},{3,2},{4,5},{5,4},{6,7},{7,6},{8,9},{9,8},{10,11... | collective-permute-start | bytes 6291464 | tf_op jit(solution)/shard_map/ppermute | solution.py:15
  1526.8 16.7 collective-permute-start.3
  1539.3 116.0 %reduce-scatter.23.cloned.1.call-start = ((), (), s32[]{:S(2)}) async-start(), calls=%async_computation.24 | async-start | bytes 983040 | tf_op jit(solution)/shard_map/reduce_scatter | solution.py:361
  1568.5 310.1 %reduce-scatter.17.cloned.1.call-start = ((), (), s32[]{:S(2)}) async-start(), calls=%async_computation.20 | async-start | bytes 18874368 | tf_op jit(solution)/shard_map/reduce_scatter | solution.py:345
  1579.2 585.4 %reduce-scatter.21.cloned.1.call-start = ((), (), s32[]{:S(2)}) async-start(), calls=%async_computation.23 | async-start | bytes 18874368 | tf_op jit(solution)/shard_map/reduce_scatter | solution.py:345
  1589.9 860.1 %reduce-scatter.15.cloned.1.call-start = ((), (), s32[]{:S(2)}) async-start(), calls=%async_computation.19 | async-start | bytes 18874368 | tf_op jit(solution)/shard_map/reduce_scatter | solution.py:344
  1601.2 1134.7 %reduce-scatter.19.cloned.1.call-start = ((), (), s32[]{:S(2)}) async-start(), calls=%async_computation.22 | async-start | bytes 18874368 | tf_op jit(solution)/shard_map/reduce_scatter | solution.py:344
  1611.6 1409.8 %reduce-scatter.13.cloned.1.call-start = ((), (), s32[]{:S(2)}) async-start(), calls=%async_computation.17 | async-start | bytes 18874368 | tf_op jit(solution)/shard_map/reduce_scatter | solution.py:220
  1626.5 1680.8 %reduce-scatter.11.cloned.1.call-start = ((), (), s32[]{:S(2)}) async-start(), calls=%async_computation.14 | async-start | bytes 18874368 | tf_op jit(solution)/shard_map/reduce_scatter | solution.py:220
  1642.7 1093.2 %copy-start.2 = (bf16[8,128,1024]{2,1,0:T(8,128)(2,1)S(1)}, bf16[8,128,1024]{2,1,0:T(8,128)(2,1)}, u32[]{:S(2)}) copy-start(bf16[8,128,1024]{2,1,0:T(8,128)(2,1)} %param.20) | copy-start | bytes 6291460
  1642.8 1093.2 %copy-start.48 = (f32[1,1024]{1,0:T(1,128)S(1)}, f32[1,1024]{1,0:T(1,128)}, u32[]{:S(2)}) copy-start(f32[1,1024]{1,0:T(1,128)} %copy-done.47) | copy-start | bytes 12292
  (134 other events, 9047.7 us)
Sparse Core Ops, SparseCore 0:
  17.2 127.5 all-gather.8
  147.6 123.0 all-gather.16
  272.9 123.0 all-gather.20
  397.5 14.9 all-gather.12
  414.5 124.8 all-gather.18
  541.5 123.0 all-gather.10
  666.8 123.0 all-gather.22
  791.4 15.0 all-gather.14
  848.0 24.8 reduce-scatter.26
  875.5 24.8 reduce-scatter.28
  1539.4 20.1 reduce-scatter.24
  1568.7 23.3 reduce-scatter.22
  1595.8 282.7 reduce-scatter.16
  1882.7 281.7 reduce-scatter.20
  2168.1 281.8 reduce-scatter.14
  2454.1 281.7 reduce-scatter.18
  2739.6 281.8 reduce-scatter.12
  3025.5 281.7 reduce-scatter.10
where the time goes:
time: 3370 us; the launch traced here: 3360 us
  waiting for transfers between devices  2290 us (68%)
  matrix products  608 us (18%)
  other arithmetic  278 us (8%)
  local copies, waits for them, and re-layouts  108 us (3%)
  blocking collectives  62.5 us (2%)
    reduce_scatter x2, waiting for transfers between devices, body(): lax.psum_scatter(grad_first, 'tensor', scatter_dimension=1, tiled=True)  571 us
    reduce_scatter x2, waiting for transfers between devices, body(): lax.psum_scatter(partial_value.reshape(seq_block, gathered_len, feature_c...  564 us
    reduce_scatter x2, waiting for transfers between devices, body(): lax.psum_scatter(grad_second, 'tensor', scatter_dimension=1, tiled=True)  507 us
    all_gather x2, waiting for transfers between devices, body(): second_norm = lax.all_gather(second_part, 'tensor', axis=1, tiled=True)  234 us
    all_gather x2, waiting for transfers between devices, body(): first_norm = lax.all_gather(first_part, 'tensor', axis=1, tiled=True)  210 us
    all_gather x2, waiting for transfers between devices, body(): dy_whole = lax.all_gather(rows_dy, 'tensor', axis=1, tiled=True)  190 us
    dot_general x16, matrix products, masked_scores(): jnp.einsum('qhe,khe->hqk', query_seq, key_seq, preferred_element_type=jnp...  109 us
    convert_element_type x8, other arithmetic, attend_back(): grad_score = (prob_full * (grad_prob - jnp.sum(prob_full * grad_prob, axi...  104 us
  transfers between devices with their start and end apart: 22, of which 13 were waited for; matrix products, arithmetic and copies ran while one was open for 29% of the time, Pallas kernels for 0%

commit v1 on v0

v1 whole, which is shorter than its diff:
```python
import functools

import jax
import jax.numpy as jnp
from jax import lax
from jax.experimental import pallas as pl
from jax.experimental.pallas import tpu as pltpu
from jax.sharding import PartitionSpec as P

HD = 64
ROT = 16
PAIR = 2 * HD
TILE = 256
SPAN = 1024
EVERY = ("fsdp", "tensor", "ctx")
CHIPS = ("fsdp", "tensor")
BF = jnp.bfloat16
F32 = jnp.float32
epsilon = 1e-05
VMEM = 56 * 1024 * 1024


def nt(a, b):
    return lax.dot_general(a, b, (((1,), (1,)), ((), ())), preferred_element_type=F32)


def nn(a, b):
    return jnp.dot(a, b, preferred_element_type=F32)


def tn(a, b):
    return lax.dot_general(a, b, (((0,), (0,)), ((), ())), preferred_element_type=F32)


def params(*kinds):
    return pltpu.CompilerParams(dimension_semantics=kinds, vmem_limit_bytes=VMEM)


def cost(flops, moved, special=0):
    return pl.CostEstimate(flops=int(flops), bytes_accessed=int(moved), transcendentals=int(special))


def layer_stats(values):
    center = values - jnp.mean(values, axis=-1, keepdims=True)
    inverse = lax.rsqrt(jnp.mean(center * center, axis=-1, keepdims=True) + epsilon)
    return (center * inverse, inverse)


def norms_kernel(x_ref, gain_ref, shift_ref, one_ref, two_ref):
    normed, _ = layer_stats(x_ref[...].astype(F32))
    one_ref[...] = (normed * gain_ref[0:1, :] + shift_ref[0:1, :]).astype(BF)
    two_ref[...] = (normed * gain_ref[1:2, :] + shift_ref[1:2, :]).astype(BF)


def norms_call(x, gains, shifts):
    tokens, feats = x.shape
    row = pl.BlockSpec((TILE, feats), lambda i: (i, 0))
    pair = pl.BlockSpec((2, feats), lambda i: (0, 0))
    return pl.pallas_call(
        norms_kernel,
        grid=(tokens // TILE,),
        in_specs=[row, pair, pair],
        out_specs=[row, row],
        out_shape=[jax.ShapeDtypeStruct((tokens, feats), BF)] * 2,
        compiler_params=params("arbitrary"),
        cost_estimate=cost(tokens * feats * 12, tokens * feats * 6),
        name="norms",
    )(x, gains, shifts)


def qkv_kernel(one_ref, w_ref, bias_ref, cos_ref, sin_ref, out_ref):
    width = w_ref.shape[0] // 3
    lane = lax.broadcasted_iota(jnp.int32, (TILE, PAIR), 1) % HD
    low_half = lane < ROT // 2
    cosine = cos_ref[...]
    sine_part = sin_ref[...]
    rows = one_ref[...]
    for part in range(3):
        span = slice(part * width, (part + 1) * width)
        whole = nt(rows, w_ref[span, :]) + bias_ref[:, span]
        if part == 2:
            out_ref[:, span] = whole.astype(BF)
            continue
        for first in range(0, width, PAIR):
            u = whole[:, first : first + PAIR]
            turned = jnp.where(
                low_half, pltpu.roll(u, PAIR - ROT // 2, 1), pltpu.roll(u, ROT // 2, 1)
            )
            u = u * cosine + turned * sine_part
            if part == 0:
                u = u * HD ** (-0.5)
            out_ref[:, part * width + first : part * width + first + PAIR] = u.astype(BF)


def qkv_call(one, w, bias, cosine, sine_part):
    tokens, feats = one.shape
    cols = w.shape[0]
    return pl.pallas_call(
        qkv_kernel,
        grid=(tokens // TILE,),
        in_specs=[
            pl.BlockSpec((TILE, feats), lambda i: (i, 0)),
            pl.BlockSpec((cols, feats), lambda i: (0, 0)),
            pl.BlockSpec((1, cols), lambda i: (0, 0)),
            pl.BlockSpec((TILE, PAIR), lambda i: (i, 0)),
            pl.BlockSpec((TILE, PAIR), lambda i: (i, 0)),
        ],
        out_specs=pl.BlockSpec((TILE, cols), lambda i: (i, 0)),
        out_shape=jax.ShapeDtypeStruct((tokens, cols), BF),
        compiler_params=params("arbitrary"),
        cost_estimate=cost(2 * tokens * feats * cols, 2 * (tokens * (feats + cols) + feats * cols)),
        name="qkv",
    )(one, w, bias, cosine, sine_part)


def turn_back(g, cosine, sine_part):
    eight = ROT // 2
    parts = []
    for head in range(2):
        own = g[head * HD : (head + 1) * HD]
        low, high = own[:eight], own[eight:ROT]
        parts += [low * cosine + high * sine_part, high * cosine - low * sine_part, own[ROT:]]
    return jnp.concatenate(parts, axis=0)


def attend_kernel(
    begin_ref,
    q_ref,
    k_ref,
    v_ref,
    grad_ref,
    doc_ref,
    cos_ref,
    sin_ref,
    att_ref,
    dq_ref,
    dk_ref,
    dv_ref,
    score_ref,
    prob_ref,
    key_turn_ref,
    value_turn_ref,
    dk_sum_ref,
    dv_sum_ref,
):
    tile = pl.program_id(1)
    tiles = pl.num_programs(1)
    total_tiles = k_ref.shape[0] // TILE

    @pl.when(tile == 0)
    def _():
        dk_sum_ref[...] = jnp.zeros_like(dk_sum_ref)
        dv_sum_ref[...] = jnp.zeros_like(dv_sum_ref)

        def turn(block, _):
            rows = pl.ds(pl.multiple_of(block * TILE, TILE), TILE)
            key_turn_ref[block] = k_ref[rows, :].astype(F32).T.astype(BF)
            value_turn_ref[block] = v_ref[rows, :].astype(F32).T.astype(BF)
            return 0

        lax.fori_loop(0, total_tiles, turn, 0)

    lane = lax.broadcasted_iota(jnp.int32, (TILE, PAIR), 1)
    q_wide = q_ref[...].astype(F32)
    g_wide = grad_ref[...].astype(F32)
    q_heads = [
        jnp.where(lane < HD, q_wide, 0.0).astype(BF),
        jnp.where(lane >= HD, q_wide, 0.0).astype(BF),
    ]
    g_heads = [
        jnp.where(lane < HD, g_wide, 0.0).astype(BF),
        jnp.where(lane >= HD, g_wide, 0.0).astype(BF),
    ]
    first = begin_ref[tile]
    doc = doc_ref[0]
    key_place = lax.broadcasted_iota(jnp.int32, (TILE, TILE), 0)
    query_place = lax.broadcasted_iota(jnp.int32, (TILE, TILE), 1) + tile * TILE

    def rows_of(block):
        return pl.ds(pl.multiple_of(block * TILE, TILE), TILE)

    def scores_step(block, tops):
        keys = k_ref[rows_of(block), :]
        place = key_place + block * TILE
        allowed = (place >= doc) & (place <= query_place)
        new = []
        for head in range(2):
            s = jnp.where(allowed, nt(keys, q_heads[head]), -1e30)
            score_ref[head, rows_of(block - first), :] = s
            new.append(jnp.maximum(tops[head], jnp.max(s, axis=0, keepdims=True)))
        return tuple(new)

    lowest = jnp.full((1, TILE), -1e30, F32)
    tops = lax.fori_loop(first, tile + 1, scores_step, (lowest, lowest))

    def exp_step(block, sums):
        values = v_ref[rows_of(block), :]
        new = []
        for head in range(2):
            e = jnp.exp(score_ref[head, rows_of(block - first), :] - tops[head])
            score_ref[head, rows_of(block - first), :] = e
            gp = nt(values, g_heads[head])
            prob_ref[head, rows_of(block - first), :] = gp
            new.append(sums[2 * head] + jnp.sum(e, axis=0, keepdims=True))
            new.append(sums[2 * head + 1] + jnp.sum(e * gp, axis=0, keepdims=True))
        return tuple(new)

    none = jnp.zeros((1, TILE), F32)
    sums = lax.fori_loop(first, tile + 1, exp_step, (none,) * 4)
    inverse = [1.0 / sums[0], 1.0 / sums[2]]
    means = [sums[1] * inverse[0], sums[3] * inverse[1]]

    def grad_step(block, turned):
        new = []
        dk = dk_sum_ref[rows_of(block), :]
        dv = dv_sum_ref[rows_of(block), :]
        for head in range(2):
            p = score_ref[head, rows_of(block - first), :] * inverse[head]
            gs = (p * (prob_ref[head, rows_of(block - first), :] - means[head])).astype(BF)
            p_low = p.astype(BF)
            dv = dv + nn(p_low, g_heads[head])
            dk = dk + nn(gs, q_heads[head])
            half = slice(head * HD, (head + 1) * HD)
            new.append(turned[2 * head] + nn(value_turn_ref[block, half, :], p_low))
            new.append(turned[2 * head + 1] + nn(key_turn_ref[block, half, :], gs))
        dk_sum_ref[rows_of(block), :] = dk
        dv_sum_ref[rows_of(block), :] = dv
        return tuple(new)

    flat = jnp.zeros((HD, TILE), F32)
    turned = lax.fori_loop(first, tile + 1, grad_step, (flat,) * 4)
    att_ref[...] = jnp.concatenate([turned[0], turned[2]], axis=0).T.astype(BF)
    dq = jnp.concatenate([turned[1], turned[3]], axis=0) * HD ** (-0.5)
    dq_ref[...] = turn_back(dq, cos_ref[tile], sin_ref[tile]).T.astype(BF)

    @pl.when(tile == tiles - 1)
    def _():
        dv_ref[...] = dv_sum_ref[...].astype(BF)

        def finish(block, _):
            g = dk_sum_ref[rows_of(block), :].T
            dk_ref[rows_of(block), :] = turn_back(g, cos_ref[block], sin_ref[block]).T.astype(BF)
            return 0

        lax.fori_loop(0, total_tiles, finish, 0)


def attend_call(begin, qkv, grad_att, doc, cosine, sine_part):
    tokens = qkv.shape[0]
    width = qkv.shape[1] // 3
    pairs = width // PAIR
    tiles = tokens // TILE
    reach = SPAN + TILE
    query = pl.BlockSpec((TILE, PAIR), lambda p, i, *_: (i, p))
    whole = pl.BlockSpec((tokens, PAIR), lambda p, i, *_: (0, p))
    table = pl.BlockSpec((tiles, ROT // 2, TILE), lambda p, i, *_: (0, 0, 0))
    return pl.pallas_call(
        attend_kernel,
        grid_spec=pltpu.PrefetchScalarGridSpec(
            num_scalar_prefetch=1,
            grid=(pairs, tiles),
            in_specs=[
                query,
                pl.BlockSpec((tokens, PAIR), lambda p, i, *_: (0, pairs + p)),
                pl.BlockSpec((tokens, PAIR), lambda p, i, *_: (0, 2 * pairs + p)),
                query,
                pl.BlockSpec((1, 1, TILE), lambda p, i, *_: (i, 0, 0)),
                table,
                table,
            ],
            out_specs=[query, query, whole, whole],
            scratch_shapes=[
                pltpu.VMEM((2, reach, TILE), F32),
                pltpu.VMEM((2, reach, TILE), F32),
                pltpu.VMEM((tiles, PAIR, TILE), BF),
                pltpu.VMEM((tiles, PAIR, TILE), BF),
                pltpu.VMEM((tokens, PAIR), F32),
                pltpu.VMEM((tokens, PAIR), F32),
            ],
        ),
        out_shape=[jax.ShapeDtypeStruct((tokens, width), BF)] * 4,
        compiler_params=params("arbitrary", "arbitrary"),
        cost_estimate=cost(
            tokens * 800 * width * 4 * 12, tokens * width * 16, tokens * 600 * (width // HD)
        ),
        name="attend",
    )(begin, qkv, qkv, qkv, grad_att, doc, cosine, sine_part)


def units_kernel(two_ref, dy_ref, win_ref, wout_ref, bias_ref, act_ref, pre_ref, sum_ref):
    pre = nt(two_ref[...], win_ref[...]) + bias_ref[...]
    upstream = nt(dy_ref[...], wout_ref[...])
    cdf = 0.5 * (1.0 + lax.erf(pre * 0.7071067811865476))
    density = jnp.exp(-0.5 * pre * pre) * 0.3989422804014327
    act_ref[...] = (pre * cdf).astype(BF)
    back = (upstream * (cdf + pre * density)).astype(BF)
    pre_ref[...] = back

    @pl.when(pl.program_id(1) == 0)
    def _():
        sum_ref[...] = jnp.zeros_like(sum_ref)

    sum_ref[...] += jnp.sum(back.astype(F32), axis=0, keepdims=True)


def units_call(two, dy, w_in, w_out, bias):
    tokens, feats = two.shape
    units = w_in.shape[0]
    step = 512
    row = pl.BlockSpec((TILE, feats), lambda j, i: (i, 0))
    weight = pl.BlockSpec((step, feats), lambda j, i: (j, 0))
    line = pl.BlockSpec((1, step), lambda j, i: (0, j))
    out = pl.BlockSpec((TILE, step), lambda j, i: (i, j))
    return pl.pallas_call(
        units_kernel,
        grid=(units // step, tokens // TILE),
        in_specs=[row, row, weight, weight, line],
        out_specs=[out, out, line],
        out_shape=[
            jax.ShapeDtypeStruct((tokens, units), BF),
            jax.ShapeDtypeStruct((tokens, units), BF),
            jax.ShapeDtypeStruct((1, units), F32),
        ],
        compiler_params=params("arbitrary", "arbitrary"),
        cost_estimate=cost(
            4 * tokens * feats * units, 40 * tokens * feats, 2 * tokens * units
        ),
        name="units",
    )(two, dy, w_in, w_out, bias)


def output_kernel(att_ref, act_ref, wd_ref, wout_ref, out_ref):
    out_ref[...] = (nn(att_ref[...], wd_ref[...]) + nn(act_ref[...], wout_ref[...])).astype(BF)


def output_call(att, act, w_dense, w_out):
    tokens, width = att.shape
    units, feats = w_out.shape
    return pl.pallas_call(
        output_kernel,
        grid=(tokens // TILE,),
        in_specs=[
            pl.BlockSpec((TILE, width), lambda i: (i, 0)),
            pl.BlockSpec((TILE, units), lambda i: (i, 0)),
            pl.BlockSpec((width, feats), lambda i: (0, 0)),
            pl.BlockSpec((units, feats), lambda i: (0, 0)),
        ],
        out_specs=pl.BlockSpec((TILE, feats), lambda i: (i, 0)),
        out_shape=jax.ShapeDtypeStruct((tokens, feats), BF),
        compiler_params=params("arbitrary"),
        cost_estimate=cost(
            2 * tokens * feats * (width + units),
            2 * (tokens * (width + units + feats) + feats * (width + units)),
        ),
        name="output",
    )(att, act, w_dense, w_out)


def back_kernel(
    dq_ref, dk_ref, dv_ref, pre_ref, x_ref, wq_ref, win_ref, gain_ref, out_ref, stat_ref, bias_ref
):
    width = dq_ref.shape[1]
    parts = [dq_ref[...], dk_ref[...], dv_ref[...]]
    one = nn(parts[0], wq_ref[:width, :])
    one += nn(parts[1], wq_ref[width : 2 * width, :])
    one += nn(parts[2], wq_ref[2 * width :, :])
    two = nn(pre_ref[...], win_ref[...])
    normed, _ = layer_stats(x_ref[...].astype(F32))
    out_ref[...] = (one * gain_ref[0:1, :] + two * gain_ref[1:2, :]).astype(BF)

    @pl.when(pl.program_id(0) == 0)
    def _():
        stat_ref[...] = jnp.zeros_like(stat_ref)
        bias_ref[...] = jnp.zeros_like(bias_ref)

    for row, value in enumerate((one * normed, two * normed, one, two)):
        stat_ref[row : row + 1, :] += jnp.sum(value, axis=0, keepdims=True)
    for row in range(3):
        span = slice(row * width, (row + 1) * width)
        bias_ref[:, span] += jnp.sum(parts[row].astype(F32), axis=0, keepdims=True)


def back_call(dq, dk, dv, pre, x, wq, w_in, gains):
    tokens, width = dq.shape
    units, feats = w_in.shape
    part = pl.BlockSpec((TILE, width), lambda i: (i, 0))
    return pl.pallas_call(
        back_kernel,
        grid=(tokens // TILE,),
        in_specs=[
            part,
            part,
            part,
            pl.BlockSpec((TILE, units), lambda i: (i, 0)),
            pl.BlockSpec((TILE, feats), lambda i: (i, 0)),
            pl.BlockSpec((3 * width, feats), lambda i: (0, 0)),
            pl.BlockSpec((units, feats), lambda i: (0, 0)),
            pl.BlockSpec((2, feats), lambda i: (0, 0)),
        ],
        out_specs=[
            pl.BlockSpec((TILE, feats), lambda i: (i, 0)),
            pl.BlockSpec((4, feats), lambda i: (0, 0)),
            pl.BlockSpec((1, 3 * width), lambda i: (0, 0)),
        ],
        out_shape=[
            jax.ShapeDtypeStruct((tokens, feats), BF),
            jax.ShapeDtypeStruct((4, feats), F32),
            jax.ShapeDtypeStruct((1, 3 * width), F32),
        ],
        compiler_params=params("arbitrary"),
        cost_estimate=cost(
            2 * tokens * feats * (3 * width + units),
            2 * (tokens * (3 * width + units + 2 * feats) + feats * (3 * width + units)),
        ),
        name="back",
    )(dq, dk, dv, pre, x, wq, w_in, gains)


def body(
    hidden_in,
    segment_ids,
    norm_gains,
    norm_biases,
    qkv_weight,
    qkv_bias,
    dense_weight,
    fc_in_weight,
    fc_in_bias,
    fc_out_weight,
    out_biases,
    out_grad,
):
    chips = lax.axis_size("tensor")
    rows_of_chips = lax.axis_size("fsdp")
    tensor_index = lax.axis_index("tensor")
    core = lax.axis_index("ctx")
    local_seqs, span, feats = hidden_in.shape
    sharing = chips // local_seqs
    ranks = 2 * sharing
    tokens = 2 * chips * span
    tiles = tokens // TILE
    local_heads = qkv_bias.shape[0]
    local_units = fc_in_bias.shape[0]
    cols = qkv_weight.shape[0]
    own_seq = tensor_index // sharing
    rank = (tensor_index % sharing) * 2 + core
    swap = sharing == 1 and local_heads % 2 == 0
    heads = chips * local_heads // ranks
    units = chips * local_units // ranks
    gains = norm_gains.astype(F32)
    shifts = norm_biases.astype(F32)
    other_core = [(0, 1), (1, 0)]

    def both_cores(own, axis):
        far = lax.ppermute(own, "ctx", other_core)
        return jnp.where(
            core == 0, jnp.stack([own, far], axis=axis), jnp.stack([far, own], axis=axis)
        )

    def to_sequence(rows):
        if sharing > 1:
            rows = jnp.repeat(rows, sharing, axis=0)
        own = lax.all_to_all(rows, "tensor", 0, 0, tiled=True)
        return own, both_cores(own, 1).reshape(tokens, feats)

    def from_sequence(rows):
        rows = lax.all_to_all(rows, "tensor", 0, 0, tiled=True)
        if sharing > 1:
            rows = rows.reshape(local_seqs, sharing, span, feats).astype(F32)
            rows = jnp.sum(rows, axis=1).astype(BF)
        return rows

    def fold_cores(part):
        blocks = part.reshape(chips, 2, span, feats)
        own = lax.dynamic_index_in_dim(blocks, core, 1, keepdims=False)
        far = lax.dynamic_index_in_dim(blocks, 1 - core, 1, keepdims=False)
        return own.astype(F32) + lax.ppermute(far, "ctx", other_core).astype(F32)

    def gather_rows(shard):
        pieces, rows, _ = shard.shape
        if swap:
            mine = lax.all_to_all(shard, "ctx", 0, 0, tiled=False)
            mine = mine.transpose(1, 0, 2).reshape(rows, 2 * cols)
            full = lax.all_gather(mine, CHIPS, axis=0, tiled=False)
            full = full.reshape(rows_of_chips, chips, rows, 2 * cols)
            return full.transpose(1, 2, 0, 3).reshape(chips, rows, feats)
        full = lax.all_gather(shard.reshape(pieces * rows, cols), EVERY, axis=0, tiled=False)
        full = full.reshape(rows_of_chips, chips, 2, pieces, rows, cols)
        full = full.transpose(1, 3, 4, 0, 2, 5).reshape(chips * pieces, rows, feats)
        count = chips * pieces // ranks
        return lax.dynamic_slice_in_dim(full, rank * count, count, 0)

    def scatter_rows(full, pieces):
        count, rows, _ = full.shape
        full = full.astype(BF)
        if swap:
            full = full.reshape(chips, rows, rows_of_chips, 2 * cols).transpose(2, 0, 1, 3)
            full = full.reshape(rows_of_chips * chips, rows, 2 * cols)
            mine = lax.psum_scatter(full, CHIPS, scatter_dimension=0, tiled=True)
            mine = mine.reshape(rows, 2, cols).transpose(1, 0, 2)
            return lax.all_to_all(mine, "ctx", 0, 0, tiled=False).astype(F32)
        wide = jnp.zeros((chips * pieces, rows, feats), BF)
        wide = lax.dynamic_update_slice_in_dim(wide, full, rank * count, 0)
        wide = wide.reshape(chips, pieces, rows, rows_of_chips, 2, cols)
        wide = wide.transpose(3, 0, 4, 1, 2, 5).reshape(-1, pieces * rows, cols)
        mine = lax.psum_scatter(wide, EVERY, scatter_dimension=0, tiled=True)
        return mine.reshape(pieces, rows, cols).astype(F32)

    def own_pieces(full):
        pieces = full.shape[1]
        if swap:
            return lax.dynamic_index_in_dim(full, core, 1, keepdims=False)
        full = full.reshape((chips * pieces,) + full.shape[2:])
        count = chips * pieces // ranks
        return lax.dynamic_slice_in_dim(full, rank * count, count, 0)

    def place_pieces(part, pieces):
        size = part.shape[1]
        if swap:
            wide = jnp.zeros((chips, pieces, size), F32)
            return lax.dynamic_update_slice_in_dim(wide, part[:, None], core, 1)
        wide = jnp.zeros((chips * pieces, size), F32)
        wide = lax.dynamic_update_slice_in_dim(wide, part, rank * part.shape[0], 0)
        return wide.reshape(chips, pieces, size)

    unit_pieces = 2 if swap else local_heads
    unit_rows = local_units // unit_pieces
    head_pieces = 2 if swap else local_heads
    head_rows = local_heads // head_pieces

    own_x, x = to_sequence(hidden_in)
    own_dy, dy = to_sequence(out_grad)
    bias_vector = jnp.concatenate([qkv_bias.reshape(-1), fc_in_bias]).astype(F32)
    bias_all = lax.all_gather(bias_vector, "tensor", axis=0, tiled=False)
    qkv_shift = own_pieces(
        bias_all[:, : local_heads * 3 * HD].reshape(chips, head_pieces, head_rows * 3 * HD)
    )
    qkv_shift = qkv_shift.reshape(heads, 3, HD).transpose(1, 0, 2).reshape(1, -1)
    unit_shift = own_pieces(
        bias_all[:, local_heads * 3 * HD :].reshape(chips, unit_pieces, unit_rows)
    ).reshape(1, units)

    w_in = gather_rows(fc_in_weight.T.reshape(unit_pieces, unit_rows, cols))
    w_in = w_in.reshape(units, feats)
    w_out = gather_rows(fc_out_weight.reshape(unit_pieces, unit_rows, cols))
    w_out = w_out.reshape(units, feats)
    w_qkv = gather_rows(
        qkv_weight.transpose(1, 2, 0).reshape(head_pieces, head_rows * 3 * HD, cols)
    )
    w_qkv = w_qkv.reshape(heads, 3, HD, feats).transpose(1, 0, 2, 3).reshape(heads * 3 * HD, feats)
    w_dense = gather_rows(dense_weight.reshape(head_pieces, head_rows * HD, cols))
    w_dense = w_dense.reshape(heads * HD, feats)

    segments = lax.dynamic_index_in_dim(segment_ids, own_seq, 0, keepdims=False)
    places = lax.broadcasted_iota(jnp.int32, (tokens,), 0)
    change = jnp.concatenate(
        [jnp.ones((1,), jnp.int32), (segments[1:] != segments[:-1]).astype(jnp.int32)]
    )
    starts = lax.cummax(places * change, axis=0)
    begin = starts[::TILE] // TILE
    freqs = 10000.0 ** (-jnp.arange(0, ROT, 2, dtype=F32) / ROT)
    angle = (places - starts).astype(F32)[:, None] * freqs
    cos_own, sin_own = jnp.cos(angle), jnp.sin(angle)
    rest = jnp.zeros((tokens, HD - ROT), F32)
    cos_lanes = jnp.concatenate([cos_own, cos_own, rest + 1.0] * 2, axis=1)
    sin_lanes = jnp.concatenate([-sin_own, sin_own, rest] * 2, axis=1)
    cos_rows = cos_own.reshape(tiles, TILE, ROT // 2).transpose(0, 2, 1)
    sin_rows = sin_own.reshape(tiles, TILE, ROT // 2).transpose(0, 2, 1)

    one, two = norms_call(x, gains, shifts)
    active, grad_pre, unit_sum = units_call(two, dy, w_in, w_out, unit_shift)
    grad_w_in = tn(grad_pre, two)
    grad_w_out = tn(active, dy)
    grad_w_in = scatter_rows(grad_w_in.reshape(-1, unit_rows, feats), unit_pieces)
    grad_w_out = scatter_rows(grad_w_out.reshape(-1, unit_rows, feats), unit_pieces)

    qkv = qkv_call(one, w_qkv, qkv_shift, cos_lanes, sin_lanes)
    grad_att = nt(dy, w_dense).astype(BF)
    attended, dq, dk, dv = attend_call(
        begin, qkv, grad_att, starts.reshape(tiles, 1, TILE), cos_rows, sin_rows
    )
    grad_w_dense = scatter_rows(
        tn(attended, dy).reshape(-1, head_rows * HD, feats), head_pieces
    )

    part = fold_cores(output_call(attended, active, w_dense, w_out))
    bias_rows = out_biases.astype(F32)
    wide_x = own_x.astype(F32)
    residual = wide_x + bias_rows[0] + bias_rows[1]
    upstream = own_dy.astype(F32)
    if sharing > 1:
        leader = tensor_index % sharing == 0
        residual = jnp.where(leader, residual, 0.0)
        upstream = jnp.where(leader, upstream, 0.0)
    hidden_out = from_sequence((residual + part).astype(BF))

    back, stats, qkv_sum = back_call(dq, dk, dv, grad_pre, x, w_qkv, w_in, gains)
    grad_w_qkv = jnp.stack([tn(g, one).astype(BF) for g in (dq, dk, dv)])
    grad_w_qkv = grad_w_qkv.reshape(3, heads, HD, feats).transpose(1, 0, 2, 3)
    grad_w_qkv = scatter_rows(grad_w_qkv.reshape(-1, head_rows * 3 * HD, feats), head_pieces)

    e = fold_cores(back)
    normed, inverse = layer_stats(wide_x)
    through = inverse * (
        e
        - jnp.mean(e, axis=-1, keepdims=True)
        - normed * jnp.mean(e * normed, axis=-1, keepdims=True)
    )
    input_grad = from_sequence((upstream + through).astype(BF))

    qkv_sum = qkv_sum.reshape(3, heads, HD).transpose(1, 0, 2).reshape(-1, head_rows * 3 * HD)
    qkv_sum = place_pieces(qkv_sum, head_pieces)
    unit_sum = place_pieces(unit_sum.reshape(-1, unit_rows), unit_pieces)
    out_sum = jnp.sum(out_grad.astype(F32), axis=(0, 1))
    packed = jnp.concatenate(
        [stats.reshape(-1), out_sum, qkv_sum.reshape(-1), unit_sum.reshape(-1)]
    )
    packed = lax.psum(packed, EVERY)
    sums = packed[: 5 * feats].reshape(5, feats)
    qkv_size = chips * local_heads * 3 * HD
    qkv_all = packed[5 * feats : 5 * feats + qkv_size].reshape(chips, local_heads, 3 * HD)
    unit_all = packed[5 * feats + qkv_size :].reshape(chips, local_units)
    grad_qkv_b = lax.dynamic_index_in_dim(qkv_all, tensor_index, 0, keepdims=False)
    grad_unit_b = lax.dynamic_index_in_dim(unit_all, tensor_index, 0, keepdims=False)
    return (
        hidden_out,
        input_grad,
        sums[0:2],
        sums[2:4],
        grad_w_qkv.reshape(local_heads, 3 * HD, cols).transpose(2, 0, 1),
        grad_qkv_b,
        grad_w_dense.reshape(local_heads, HD, cols),
        grad_w_in.reshape(local_units, cols).T,
        grad_unit_b,
        grad_w_out.reshape(local_units, cols),
        jnp.stack([sums[4], sums[4]]),
    )


def solution(mesh):
    rows = P("fsdp", ("tensor", "ctx"), None)
    weights = (
        P(("fsdp", "ctx"), "tensor", None),
        P("tensor", None),
        P("tensor", None, ("fsdp", "ctx")),
        P(("fsdp", "ctx"), "tensor"),
        P("tensor"),
        P("tensor", ("fsdp", "ctx")),
    )
    return jax.shard_map(
        body,
        mesh=mesh,
        in_specs=(rows, P("fsdp", None), P(), P()) + weights + (P(), rows),
        out_specs=(rows, rows, P(), P()) + weights + (P(),),
        check_vma=False,
    )
```

time: 3370 us -> 852 us (0.25)
  waiting for transfers between devices: 2290 us -> 144 us
  matrix products: 608 us -> 44.1 us
  other arithmetic: 278 us -> 31.8 us
  blocking collectives: 62.5 us -> 284 us
  Pallas kernels: 0 us -> 186 us
    reduce_scatter x10 -> x4, waiting for transfers between devices: 1640 us -> 89.8 us  [scatter_rows(): mine = lax.psum_scatter(full, CHIPS, scatter_dimension=0, tiled=True)]
    all_gather x8 -> x4, waiting for transfers between devices: 640 us -> 0.01 us  [gather_rows(): full = lax.all_gather(mine, CHIPS, axis=0, tiled=False)]
    dot_general x80 -> x7, matrix products: 608 us -> 44.1 us  [the longest x6 40.4 us: tn(): lax.dot_general(a, b, (((0,), (0,)), ((), ())), preferred_element_type=F32)]
    pallas_call x0 -> x6, Pallas kernels: none -> 186 us  [the longest x1 80.8 us: attend_call(): pl.pallas_call(attend_kernel, grid_spec=pltpu.PrefetchScalarGridSpec(num_...]
    all_to_all x0 -> x9, blocking collectives: none -> 168 us  [the longest x1 73.9 us: from_sequence(): rows = lax.all_to_all(rows, 'tensor', 0, 0, tiled=True)]
    convert_element_type x17 -> x6, other arithmetic: 119 us -> 8.28 us  [the longest x1 6.33 us: body(): input_grad = from_sequence((upstream + through).astype(BF))]
    all_to_all x0 -> x3, waiting for transfers between devices: none -> 54.5 us  [the longest x1 54.5 us: to_sequence(): own = lax.all_to_all(rows, 'tensor', 0, 0, tiled=True)]
    reduce_sum x12 -> x2, other arithmetic: 49 us -> 3.58 us  [the longest x1 3.22 us: body(): jnp.mean(e, axis=-1, keepdims=True)]
  transfers between devices with their start and end apart: 22 -> 15, of which waited for: 13 -> 3; matrix products, arithmetic and copies ran while one was open for 29% -> 23% of each run, Pallas kernels for 0% -> 22%
where the time goes in v1:
time: 852 us; the launch traced here: 842 us
  blocking collectives  284 us (33%)
  Pallas kernels  186 us (22%)
  waiting for transfers between devices  144 us (17%)
  local copies, waits for them, and re-layouts  124 us (15%)
  matrix products  44.1 us (5%)
  other arithmetic  31.8 us (4%)
  between operations  14.9 us (2%)
  starting transfers between devices  13.2 us (2%)
    reduce_scatter x4, waiting for transfers between devices, scatter_rows(): mine = lax.psum_scatter(full, CHIPS, scatter_dimension=0, tiled=True)  89.8 us
    psum x1, blocking collectives, body(): packed = lax.psum(packed, EVERY)  85.1 us
    pallas_call x1, Pallas kernels, attend_call(): pl.pallas_call(attend_kernel, grid_spec=pltpu.PrefetchScalarGridSpec(num_...  80.8 us
    all_to_all x1, blocking collectives, from_sequence(): rows = lax.all_to_all(rows, 'tensor', 0, 0, tiled=True)  73.9 us
    all_to_all x1, blocking collectives, to_sequence(): own = lax.all_to_all(rows, 'tensor', 0, 0, tiled=True)  64.5 us
    all_to_all x1, waiting for transfers between devices, to_sequence(): own = lax.all_to_all(rows, 'tensor', 0, 0, tiled=True)  54.5 us
    pallas_call x1, Pallas kernels, units_call(): pl.pallas_call(units_kernel, grid=(units // step, tokens // TILE), in_spe...  40.6 us
    dot_general x6, matrix products, tn(): lax.dot_general(a, b, (((0,), (0,)), ((), ())), preferred_element_type=F32)  40.4 us
  transfers between devices with their start and end apart: 15, of which 3 were waited for; matrix products, arithmetic and copies ran while one was open for 23% of the time, Pallas kernels for 22%

profile of v1, /device:TPU:0, one launch (start us, length us, event | category | flops | bytes accessed | tf_op | source)
XLA Modules:
  0.0 842.1 jit_solution(614746315249421895)
XLA Ops:
  28.9 64.5 %all_to_all.64 = bf16[8,128,1024]{2,1,0:T(8,128)(2,1)S(1)} all-to-all(bf16[8,128,1024]{2,1,0:T(8,128)(2,1)} %param.12), channel_id=1, replica_groups=mesh['fsdp'=2,'tensor'=8,'ctx'=2] {'tensor'}, dimensions={0} | all-to-all | bytes 4194304 | tf_op jit(solution)/shard_map/all_to_all | solution.py:463
  100.0 54.5 %all-to-all-done.2 = bf16[8,128,1024]{2,1,0:T(8,128)(2,1)} async-done(((bf16[8,128,1024]{2,1,0:T(8,128)(2,1)}), bf16[8,128,1024]{2,1,0:T(8,128)(2,1)}, u32[]{:S(2)}, u32[]{:S(2)}) %all-to-all-start.2) | async-done | bytes 2097184 | tf_op jit(solution)/shard_map/all_to_all | solution.py:463
  156.4 30.6 %all-gather = f32[8,1,896]{2,1,0:T(1,128)S(1)} all-gather(f32[1,1,896]{2,1,0:T(1,128)S(1)} %fusion.17), channel_id=1, replica_groups=mesh['fsdp'=2,'tensor'=8,'ctx'=2] {'tensor'}, dimensions={0}, use_global_device_ids=true | all-gather | bytes 32256 | tf_op jit(solution)/shard_map/all_gather | solution.py:534
  188.3 6.1 multiply_sine_fusion
  219.2 9.3 %norms.1 = (bf16[2048,1024]{1,0:T(8,128)(2,1)}, bf16[2048,1024]{1,0:T(8,128)(2,1)}) custom-call(bf16[2048,1024]{1,0:T(8,128)(2,1)} %bitcast.175, f32[2,1024]{1,0:T(2,128)} %convert_element_type.100.gain_ref, f32[2,1024]{1,0:T(2,128)} %convert_element_type.101.shift_ref), custom_call_target="tpu_custom_call" | custom-call | flops 25165824 | bytes 12582912 | tf_op jit(solution)/shard_map/norms/pallas_call | solution.py:59
  232.2 6.8 copy.188
  239.0 6.1 reshape_reshape.15
  249.2 12.8 %qkv.1.q_ref.k_ref.v_ref = bf16[2048,1536]{1,0:T(8,128)(2,1)} custom-call(bf16[2048,1024]{1,0:T(8,128)(2,1)} %get-tuple-element.23.one_ref, bf16[1536,1024]{1,0:T(8,128)(2,1)} %bitcast.204, f32[1,1536]{1,0:T(1,128)} %reshape.364.bias_ref, f32[2048,128]{1,0:T(8,128)} %concatenate.35.cos_ref, f32[2048,128]{1,0:T(8,128)} %concatenate.36.sin_ref), custom_call_target="tpu_custom_call" | custom-call | flops 6442450944 | bytes 13631488 | tf_op jit(solution)/shard_map/qkv/pallas_call | solution.py:98
  262.0 80.8 %attend.1 = (bf16[2048,512]{1,0:T(8,128)(2,1)}, bf16[2048,512]{1,0:T(8,128)(2,1)}, bf16[2048,512]{1,0:T(8,128)(2,1)}, bf16[2048,512]{1,0:T(8,128)(2,1)}) custom-call(s32[8]{0:T(128)} %and_select_fusion.begin_ref, bf16[2048,1536]{1,0:T(8,128)(2,1)} %qkv.1.q_ref.k_ref.v_ref, bf16[2048,1536]{1,0:T(8,128)(2,1)} %qkv.1.q_ref.k_ref.v_ref, ...), custom_call_target="tpu_custom_call" | custom-call | flops 40265318400 | bytes 16777216 | tf_op jit(solution)/shard_map/attend/pallas_call | solution.py:257
  365.2 6.2 reshape_reshape.19
  376.5 6.5 copy.142
  386.2 6.5 copy.145
  395.8 40.6 %units.1 = (bf16[2048,2048]{1,0:T(8,128)(2,1)}, bf16[2048,2048]{1,0:T(8,128)(2,1)}, f32[1,2048]{1,0:T(1,128)}) custom-call(bf16[2048,1024]{1,0:T(8,128)(2,1)} %get-tuple-element.25.two_ref, bf16[2048,1024]{1,0:T(8,128)(2,1)} %bitcast.192, bf16[2048,1024]{1,0:T(8,128)(2,1)} %bitcast.196, bf16[2048,1024]{1,0:T(8,128)(2,1)} %bitcast.194, f32[1,2048]{1,0:T(1,128)} %bitcast.245), custom_call_target="tpu_custom_call" | custom-call | flops 17179869184 | bytes 83886080 | tf_op jit(solution)/shard_map/units/pallas_call | solution.py:314
  436.4 12.7 %convolution_convert_fusion = bf16[2048,1024]{1,0:T(8,128)(2,1)} fusion(bf16[2048,2048]{1,0:T(8,128)(2,1)} %get-tuple-element.30.pre_ref, bf16[2048,1024]{1,0:T(8,128)(2,1)S(1)} %copy-done.14), kind=kOutput, calls=%fused_computation.22 | convolution fusion | flops 8592031744 | bytes 16777216 | tf_op jit(solution)/shard_map/dot_general | solution.py:32
  449.1 7.9 convert_element_type.122
  463.8 26.8 %back.1 = (bf16[2048,1024]{1,0:T(8,128)(2,1)}, f32[4,1024]{1,0:T(4,128)}, f32[1,1536]{1,0:T(1,128)}) custom-call(bf16[2048,512]{1,0:T(8,128)(2,1)} %get-tuple-element.27.dq_ref, bf16[2048,512]{1,0:T(8,128)(2,1)} %get-tuple-element.28.dk_ref, bf16[2048,512]{1,0:T(8,128)(2,1)} %get-tuple-element.29.dv_ref, bf16[2048,2048]{1,0:T(8,128)(2,1)} %get-tuple-element.30.pre_ref, ...), custom_call_target="tpu_custom_call" | custom-call | flops 15032385536 | bytes 30408704 | tf_op jit(solution)/shard_map/back/pallas_call | solution.py:387
  493.7 16.2 %output.1 = bf16[2048,1024]{1,0:T(8,128)(2,1)} custom-call(bf16[2048,512]{1,0:T(8,128)(2,1)} %get-tuple-element.24.att_ref, bf16[2048,2048]{1,0:T(8,128)(2,1)} %get-tuple-element.26.act_ref, bf16[512,1024]{1,0:T(8,128)(2,1)} %bitcast.211, bf16[2048,1024]{1,0:T(8,128)(2,1)} %bitcast.195), custom_call_target="tpu_custom_call" | custom-call | flops 10737418240 | bytes 19922944 | tf_op jit(solution)/shard_map/output/pallas_call | solution.py:339
  513.4 12.0 %copy.167 = bf16[2048,2048]{1,0:T(8,128)(2,1)} copy(bf16[2048,2048]{0,1:T(8,128)(2,1)} %bitcast.186) | data formatting | bytes 16777216 | tf_op jit(solution)/shard_map/dot_general | solution.py:32
  525.4 12.5 %convolution_convert_fusion.2 = bf16[8,256,1024]{2,1,0:T(8,128)(2,1)S(1)} fusion(bf16[8,256,2048]{2,1,0:T(8,128)(2,1)} %bitcast.187, bf16[2048,1024,1]{1,0,2:T(8,128)(2,1)} %bitcast.193), kind=kOutput, calls=%fused_computation.27 | convolution fusion | flops 8592031744 | bytes 16777216 | tf_op jit(solution)/shard_map/dot_general | solution.py:32
  548.7 6.3 fusion.8
  555.0 20.0 %reduce-scatter.5.cloned.1.call-done = bf16[1,192,512]{2,1,0:T(8,128)(2,1)} async-done(((bf16[16,192,512]{2,1,0:T(8,128)(2,1)}), bf16[1,192,512]{2,1,0:T(8,128)(2,1)}) %reduce-scatter.5.cloned.1.call-update) | async-done | bytes 196624 | tf_op jit(solution)/shard_map/reduce_scatter | solution.py:499
  579.9 73.9 %all_to_all.66 = bf16[8,128,1024]{2,1,0:T(8,128)(2,1)} all-to-all(bf16[8,128,1024]{2,1,0:T(8,128)(2,1)} %get-tuple-element.84), channel_id=1, replica_groups=mesh['fsdp'=2,'tensor'=8,'ctx'=2] {'tensor'}, dimensions={0} | all-to-all | bytes 4194304 | tf_op jit(solution)/shard_map/all_to_all | solution.py:467
  659.1 85.1 %psum.7 = f32[12288]{0:T(1024)S(1)} all-reduce(f32[12288]{0:T(1024)S(1)} %pad_maximum_fusion), channel_id=1, replica_groups=mesh['fsdp'=2,'tensor'=8,'ctx'=2] {'fsdp','tensor','ctx'}, use_global_device_ids=true, to_apply=%region_7.8 | all-reduce | flops 12288 | bytes 98304 | tf_op jit(solution)/shard_map/psum | solution.py:618
  755.0 69.8 %reduce-scatter.11.cloned.1.call-done = bf16[1,256,512]{2,1,0:T(8,128)(2,1)} async-done(((bf16[16,256,512]{2,1,0:T(8,128)(2,1)}), bf16[1,256,512]{2,1,0:T(8,128)(2,1)}) %reduce-scatter.11.cloned.1.call-update) | async-done | bytes 262160 | tf_op jit(solution)/shard_map/reduce_scatter | solution.py:499
  (189 shorter events, 152.8 us)
Async XLA Ops:
  7.2 17.8 %copy-start.5 = (bf16[512,256]{1,0:T(8,128)(2,1)S(1)}, bf16[512,256]{1,0:T(8,128)(2,1)}, u32[]{:S(2)}) copy-start(bf16[512,256]{1,0:T(8,128)(2,1)} %param.21) | copy-start | bytes 786436
  7.2 200.3 %all-gather.8.cloned.1.call-start = ((), (), s32[]{:S(2)}) async-start(), calls=%async_computation.17 | async-start | bytes 1114112 | tf_op jit(solution)/shard_map/all_gather | solution.py:484
  12.8 219.4 %all-gather.6.cloned.1.call-start = ((), (), s32[]{:S(2)}) async-start(), calls=%async_computation.16 | async-start | bytes 3342336 | tf_op jit(solution)/shard_map/all_gather | solution.py:484
  18.9 357.6 %all-gather.10.cloned.1.call-start = ((), (), s32[]{:S(2)}) async-start(), calls=%async_computation.18 | async-start | bytes 4456448 | tf_op jit(solution)/shard_map/all_gather | solution.py:484
  28.9 126.1 %copy-start.10 = (bf16[2,1024]{1,0:T(2,128)(2,1)S(1)}, bf16[2,1024]{1,0:T(2,128)(2,1)}, u32[]{:S(2)}) copy-start(bf16[2,1024]{1,0:T(2,128)(2,1)} %param.14) | copy-start | bytes 12292
  28.9 126.7 %copy-start.11 = (bf16[2,1024]{1,0:T(2,128)(2,1)S(1)}, bf16[2,1024]{1,0:T(2,128)(2,1)}, u32[]{:S(2)}) copy-start(bf16[2,1024]{1,0:T(2,128)(2,1)} %param.15) | copy-start | bytes 12292
  28.9 127.3 %copy-start.12 = (bf16[512]{0:T(512)(128)(2,1)S(1)}, bf16[512]{0:T(512)(128)(2,1)}, u32[]{:S(2)}) copy-start(bf16[512]{0:T(512)(128)(2,1)} %param.20) | copy-start | bytes 3076
  28.9 127.3 %copy-start.13 = (bf16[2,192]{1,0:T(2,128)(2,1)S(1)}, bf16[2,192]{1,0:T(2,128)(2,1)}, u32[]{:S(2)}) copy-start(bf16[2,192]{1,0:T(2,128)(2,1)} %param.17) | copy-start | bytes 2308
  93.5 61.1 %all-to-all-start.2 = ((bf16[8,128,1024]{2,1,0:T(8,128)(2,1)}), bf16[8,128,1024]{2,1,0:T(8,128)(2,1)}, u32[]{:S(2)}, u32[]{:S(2)}) async-start(bf16[8,128,1024]{2,1,0:T(8,128)(2,1)} %param.23), calls=%async_computation.2 | async-start | bytes 4194304 | tf_op jit(solution)/shard_map/all_to_all | solution.py:463
  97.8 288.4 %all-gather.12.cloned.1.call-start = ((), (), s32[]{:S(2)}) async-start(), calls=%async_computation.19 | async-start | bytes 4456448 | tf_op jit(solution)/shard_map/all_gather | solution.py:484
  98.9 441.5 %reduce-scatter.7.cloned.1.call-start = ((), (), s32[]{:S(2)}) async-start(), calls=%async_computation.21 | async-start | bytes 1114112 | tf_op jit(solution)/shard_map/reduce_scatter | solution.py:499
  100.0 110.1 %collective-permute-start = (bf16[8,128,1024]{2,1,0:T(8,128)(2,1)S(1)}, bf16[8,128,1024]{2,1,0:T(8,128)(2,1)}, u32[]{:S(2)}, u32[]{:S(2)}) collective-permute-start(bf16[8,128,1024]{2,1,0:T(8,128)(2,1)S(1)} %all_to_all.64), channel_id=1, source_target_pairs={{0,1},{1,0},{2,3},{3,2},{4,5},{5,4},{6,7},{7,6},{8,9},{9,8},{10,11... | collective-permute-start | bytes 6291464 | tf_op jit(solution)/shard_map/ppermute | solution.py:455
  154.5 55.5 %collective-permute-start.1 = (bf16[8,128,1024]{2,1,0:T(8,128)(2,1)}, bf16[8,128,1024]{2,1,0:T(8,128)(2,1)}, u32[]{:S(2)}, u32[]{:S(2)}) collective-permute-start(bf16[8,128,1024]{2,1,0:T(8,128)(2,1)} %all-to-all-done.2), channel_id=1, source_target_pairs={{0,1},{1,0},{2,3},{3,2},{4,5},{5,4},{6,7},{7,6},{8,9},{9,8},{10,11... | collective-permute-start | bytes 6291464 | tf_op jit(solution)/shard_map/ppermute | solution.py:455
  210.1 18.4 %copy-start.4 = (bf16[64,8,2,512]{3,1,2,0:T(8,128)(2,1)}, bf16[64,8,2,512]{3,1,2,0:T(8,128)(2,1)S(1)}, u32[]{:S(2)}) copy-start(bf16[64,8,2,512]{3,1,2,0:T(8,128)(2,1)S(1)} %copy.173) | copy-start | bytes 3145732
  353.1 221.9 %reduce-scatter.5.cloned.1.call-start = ((), (), s32[]{:S(2)}) async-start(), calls=%async_computation.20 | async-start | bytes 3342336 | tf_op jit(solution)/shard_map/reduce_scatter | solution.py:499
  375.6 373.2 %reduce-scatter.9.cloned.1.call-start = ((), (), s32[]{:S(2)}) async-start(), calls=%async_computation.22 | async-start | bytes 4456448 | tf_op jit(solution)/shard_map/reduce_scatter | solution.py:499
  395.8 40.6 %copy-start.14 = (bf16[2048,1024]{1,0:T(8,128)(2,1)S(1)}, bf16[2048,1024]{1,0:T(8,128)(2,1)}, u32[]{:S(2)}) copy-start(bf16[2048,1024]{1,0:T(8,128)(2,1)} %get-tuple-element.25.two_ref) | copy-start | bytes 12582916
  462.1 362.7 %reduce-scatter.11.cloned.1.call-start = ((), (), s32[]{:S(2)}) async-start(), calls=%async_computation.23 | async-start | bytes 4456448 | tf_op jit(solution)/shard_map/reduce_scatter | solution.py:499
  493.7 51.6 %collective-permute-start.3 = (bf16[8,128,1024]{2,1,0:T(8,128)(2,1)}, bf16[8,128,1024]{2,1,0:T(8,128)(2,1)}, u32[]{:S(2)}, u32[]{:S(2)}) collective-permute-start(bf16[8,128,1024]{2,1,0:T(8,128)(2,1)} %dynamic-slice_bitcast_fusion), channel_id=1, source_target_pairs={{0,1},{1,0},{2,3},{3,2},{4,5},{5,4},{6,7},{7,6},{8,9},{9,8},{10,11... | collective-permute-start | bytes 6291464 | tf_op jit(solution)/shard_map/ppermute | solution.py:477
  512.9 35.6 %collective-permute-start.2 = (bf16[8,128,1024]{2,1,0:T(8,128)(2,1)}, bf16[8,128,1024]{2,1,0:T(8,128)(2,1)}, u32[]{:S(2)}, u32[]{:S(2)}) collective-permute-start(bf16[8,128,1024]{2,1,0:T(8,128)(2,1)} %dynamic-slice_bitcast_fusion.1), channel_id=1, source_target_pairs={{0,1},{1,0},{2,3},{3,2},{4,5},{5,4},{6,7},{7,6},{8,9},{9,8},{10,11... | collective-permute-start | bytes 6291464 | tf_op jit(solution)/shard_map/ppermute | solution.py:477
  541.9 34.1 %all-to-all-start.9 = ((bf16[2,64,256]{2,1,0:T(8,128)(2,1)}), bf16[2,64,256]{2,1,0:T(8,128)(2,1)S(1)}, u32[]{:S(2)}, u32[]{:S(2)}) async-start(bf16[2,64,256]{2,1,0:T(8,128)(2,1)} %copy.158), calls=%async_computation.11 | async-start | bytes 131072 | tf_op jit(solution)/shard_map/all_to_all | solution.py:501
  579.9 78.3 %copy-start.1 = (bf16[8,128,1024]{2,1,0:T(8,128)(2,1)S(1)}, bf16[8,128,1024]{2,1,0:T(8,128)(2,1)}, u32[]{:S(2)}) copy-start(bf16[8,128,1024]{2,1,0:T(8,128)(2,1)} %param.23) | copy-start | bytes 6291460
  653.7 95.1 %all-to-all-start.7 = ((bf16[8,128,1024]{2,1,0:T(8,128)(2,1)}), bf16[8,128,1024]{2,1,0:T(8,128)(2,1)}, u32[]{:S(2)}, u32[]{:S(2)}) async-start(bf16[8,128,1024]{2,1,0:T(8,128)(2,1)} %get-tuple-element.83), calls=%async_computation.7 | async-start | bytes 4194304 | tf_op jit(solution)/shard_map/all_to_all | solution.py:467
  658.6 172.1 %copy-start.2 = (bf16[8,128,1024]{2,1,0:T(8,128)(2,1)S(1)}, bf16[8,128,1024]{2,1,0:T(8,128)(2,1)}, u32[]{:S(2)}) copy-start(bf16[8,128,1024]{2,1,0:T(8,128)(2,1)} %all_to_all.66) | copy-start | bytes 6291460
  (9 other events, 41.9 us)
Sparse Core Ops, SparseCore 0:
  13.0 65.9 all-gather.7
  82.3 93.4 all-gather.5
  179.2 74.3 all-gather.9
  256.8 74.6 all-gather.11
  353.2 88.9 reduce-scatter.6
  447.7 127.1 reduce-scatter.4
  577.4 147.5 reduce-scatter.8
  727.4 97.3 reduce-scatter.10

commit v2 on v1

v2 whole, which is shorter than its diff:
```python
import jax
import jax.numpy as jnp
from jax import lax
from jax.experimental import pallas as pl
from jax.experimental.layout import Layout, with_layout_constraint
from jax.experimental.pallas import tpu as pltpu
from jax.sharding import PartitionSpec as P

HD = 64
ROT = 16
PAIR = 2 * HD
TILE = 256
WIDE = 512
SPAN = 1024
CHIPS = ("fsdp", "tensor")
EVERY = ("fsdp", "tensor", "ctx")
BF = jnp.bfloat16
F32 = jnp.float32
epsilon = 1e-05
VMEM = 56 * 1024 * 1024


AFTER = pl.BlockSpec(memory_space=pl.ANY)


def nt(a, b):
    return lax.dot_general(a, b, (((1,), (1,)), ((), ())), preferred_element_type=F32)


def nn(a, b):
    return jnp.dot(a, b, preferred_element_type=F32)


def tn(a, b):
    return lax.dot_general(a, b, (((0,), (0,)), ((), ())), preferred_element_type=F32)


def params(*kinds):
    return pltpu.CompilerParams(dimension_semantics=kinds, vmem_limit_bytes=VMEM)


def cost(flops, moved, special=0):
    return pl.CostEstimate(flops=int(flops), bytes_accessed=int(moved), transcendentals=int(special))


def layer_stats(values):
    center = values - jnp.mean(values, axis=-1, keepdims=True)
    inverse = lax.rsqrt(jnp.mean(center * center, axis=-1, keepdims=True) + epsilon)
    return (center * inverse, inverse)


def in_order(core_ref, own_ref, far_ref):
    first = core_ref[0] == 0
    own, far = own_ref[0], far_ref[0]
    return jnp.where(first, own, far), jnp.where(first, far, own)


def merge_kernel(core_ref, own_ref, far_ref, after_ref, out_ref):
    span = own_ref.shape[1]
    low, high = in_order(core_ref, own_ref, far_ref)
    out_ref[:span, :] = low
    out_ref[span:, :] = high


def norms_kernel(core_ref, own_ref, far_ref, gain_ref, shift_ref, out_ref, one_ref, two_ref):
    span = own_ref.shape[1]
    for index, rows in enumerate(in_order(core_ref, own_ref, far_ref)):
        place = slice(index * span, (index + 1) * span)
        out_ref[place, :] = rows
        normed, _ = layer_stats(rows.astype(F32))
        one_ref[place, :] = (normed * gain_ref[0:1, :] + shift_ref[0:1, :]).astype(BF)
        two_ref[place, :] = (normed * gain_ref[1:2, :] + shift_ref[1:2, :]).astype(BF)


def merge_call(core, own, far, after=None, gains=None, shifts=None):
    blocks, span, feats = own.shape
    tokens = 2 * blocks * span
    block = pl.BlockSpec((1, span, feats), lambda i, *_: (i, 0, 0))
    row = pl.BlockSpec((2 * span, feats), lambda i, *_: (i, 0))
    pair = pl.BlockSpec((2, feats), lambda i, *_: (0, 0))
    plain = gains is None
    count = 1 if plain else 3
    return pl.pallas_call(
        merge_kernel if plain else norms_kernel,
        grid_spec=pltpu.PrefetchScalarGridSpec(
            num_scalar_prefetch=1,
            grid=(blocks,),
            in_specs=[block, block] + ([AFTER] if plain else [pair, pair]),
            out_specs=[row] * count,
        ),
        out_shape=[jax.ShapeDtypeStruct((tokens, feats), BF)] * count,
        compiler_params=params("arbitrary"),
        cost_estimate=cost(tokens * feats * 12, tokens * feats * 2 * (1 + count)),
        name="merge" if plain else "norms",
    )(*((core, own, far) + ((after,) if plain else (gains, shifts))))


def block_of(ref, side, first, count):
    rows = ref[side, :, first : first + count, :]
    return rows.reshape(-1, rows.shape[-1])


def columns(side, wide):
    return slice(side * wide, (side + 1) * wide)


def qkv_kernel(one_ref, dy_ref, w_ref, bias_ref, cos_ref, sin_ref, after_ref, out_ref, grad_ref):
    sides, groups, _, wide = w_ref.shape
    width = groups * HD
    lane = lax.broadcasted_iota(jnp.int32, (WIDE, PAIR), 1) % HD
    low_half = lane < ROT // 2
    cosine = cos_ref[...]
    sine_part = sin_ref[...]

    def product(rows_ref, part):
        return sum(
            nt(rows_ref[:, columns(f, wide)], block_of(w_ref, f, part * HD, HD))
            for f in range(sides)
        )

    for part in range(3):
        span = slice(part * width, (part + 1) * width)
        whole = product(one_ref, part) + bias_ref[:, span]
        if part == 2:
            out_ref[:, span] = whole.astype(BF)
            continue
        for first in range(0, width, PAIR):
            u = whole[:, first : first + PAIR]
            turned = jnp.where(
                low_half, pltpu.roll(u, PAIR - ROT // 2, 1), pltpu.roll(u, ROT // 2, 1)
            )
            u = u * cosine + turned * sine_part
            if part == 0:
                u = u * HD ** (-0.5)
            out_ref[:, part * width + first : part * width + first + PAIR] = u.astype(BF)
    grad_ref[...] = product(dy_ref, 3).astype(BF)


def qkv_call(one, dy, w, bias, cosine, sine_part, after):
    tokens, feats = one.shape
    width = w.shape[1] * HD
    row = lambda size: pl.BlockSpec((WIDE, size), lambda i: (i, 0))
    return pl.pallas_call(
        qkv_kernel,
        grid=(tokens // WIDE,),
        in_specs=[
            row(feats),
            row(feats),
            pl.BlockSpec(w.shape, lambda i: (0, 0, 0, 0)),
            pl.BlockSpec((1, 3 * width), lambda i: (0, 0)),
            row(PAIR),
            row(PAIR),
            AFTER,
        ],
        out_specs=[row(3 * width), row(width)],
        out_shape=[
            jax.ShapeDtypeStruct((tokens, 3 * width), BF),
            jax.ShapeDtypeStruct((tokens, width), BF),
        ],
        compiler_params=params("arbitrary"),
        cost_estimate=cost(16 * tokens * feats * width, 8 * tokens * (feats + width)),
        name="qkv",
    )(one, dy, w, bias, cosine, sine_part, after)


def turn_back(g, cosine, sine_part):
    eight = ROT // 2
    parts = []
    for head in range(2):
        own = g[head * HD : (head + 1) * HD]
        low, high = own[:eight], own[eight:ROT]
        parts += [low * cosine + high * sine_part, high * cosine - low * sine_part, own[ROT:]]
    return jnp.concatenate(parts, axis=0)


def attend_kernel(
    begin_ref,
    q_ref,
    k_ref,
    v_ref,
    grad_ref,
    doc_ref,
    cos_ref,
    sin_ref,
    att_ref,
    dq_ref,
    dk_ref,
    dv_ref,
    score_ref,
    prob_ref,
    key_turn_ref,
    value_turn_ref,
    dk_sum_ref,
    dv_sum_ref,
):
    tile = pl.program_id(1)
    tiles = pl.num_programs(1)
    total_tiles = k_ref.shape[0] // TILE

    @pl.when(tile == 0)
    def _():
        dk_sum_ref[...] = jnp.zeros_like(dk_sum_ref)
        dv_sum_ref[...] = jnp.zeros_like(dv_sum_ref)

        def turn(block, _):
            rows = pl.ds(pl.multiple_of(block * TILE, TILE), TILE)
            key_turn_ref[block] = k_ref[rows, :].astype(F32).T.astype(BF)
            value_turn_ref[block] = v_ref[rows, :].astype(F32).T.astype(BF)
            return 0

        lax.fori_loop(0, total_tiles, turn, 0)

    lane = lax.broadcasted_iota(jnp.int32, (TILE, PAIR), 1)
    q_wide = q_ref[...].astype(F32)
    g_wide = grad_ref[...].astype(F32)
    q_heads = [
        jnp.where(lane < HD, q_wide, 0.0).astype(BF),
        jnp.where(lane >= HD, q_wide, 0.0).astype(BF),
    ]
    g_heads = [
        jnp.where(lane < HD, g_wide, 0.0).astype(BF),
        jnp.where(lane >= HD, g_wide, 0.0).astype(BF),
    ]
    first = begin_ref[tile]
    doc = doc_ref[0]
    key_place = lax.broadcasted_iota(jnp.int32, (TILE, TILE), 0)
    query_place = lax.broadcasted_iota(jnp.int32, (TILE, TILE), 1) + tile * TILE

    def rows_of(block):
        return pl.ds(pl.multiple_of(block * TILE, TILE), TILE)

    def scores_step(block, tops):
        keys = k_ref[rows_of(block), :]
        place = key_place + block * TILE
        allowed = (place >= doc) & (place <= query_place)
        new = []
        for head in range(2):
            s = jnp.where(allowed, nt(keys, q_heads[head]), -1e30)
            score_ref[head, rows_of(block - first), :] = s
            new.append(jnp.maximum(tops[head], jnp.max(s, axis=0, keepdims=True)))
        return tuple(new)

    lowest = jnp.full((1, TILE), -1e30, F32)
    tops = lax.fori_loop(first, tile + 1, scores_step, (lowest, lowest))

    def exp_step(block, sums):
        values = v_ref[rows_of(block), :]
        new = []
        for head in range(2):
            e = jnp.exp(score_ref[head, rows_of(block - first), :] - tops[head])
            score_ref[head, rows_of(block - first), :] = e
            gp = nt(values, g_heads[head])
            prob_ref[head, rows_of(block - first), :] = gp
            new.append(sums[2 * head] + jnp.sum(e, axis=0, keepdims=True))
            new.append(sums[2 * head + 1] + jnp.sum(e * gp, axis=0, keepdims=True))
        return tuple(new)

    none = jnp.zeros((1, TILE), F32)
    sums = lax.fori_loop(first, tile + 1, exp_step, (none,) * 4)
    inverse = [1.0 / sums[0], 1.0 / sums[2]]
    means = [sums[1] * inverse[0], sums[3] * inverse[1]]

    def grad_step(block, turned):
        new = []
        dk = dk_sum_ref[rows_of(block), :]
        dv = dv_sum_ref[rows_of(block), :]
        for head in range(2):
            p = score_ref[head, rows_of(block - first), :] * inverse[head]
            gs = (p * (prob_ref[head, rows_of(block - first), :] - means[head])).astype(BF)
            p_low = p.astype(BF)
            dv = dv + nn(p_low, g_heads[head])
            dk = dk + nn(gs, q_heads[head])
            half = slice(head * HD, (head + 1) * HD)
            new.append(turned[2 * head] + nn(value_turn_ref[block, half, :], p_low))
            new.append(turned[2 * head + 1] + nn(key_turn_ref[block, half, :], gs))
        dk_sum_ref[rows_of(block), :] = dk
        dv_sum_ref[rows_of(block), :] = dv
        return tuple(new)

    flat = jnp.zeros((HD, TILE), F32)
    turned = lax.fori_loop(first, tile + 1, grad_step, (flat,) * 4)
    att_ref[...] = jnp.concatenate([turned[0], turned[2]], axis=0).T.astype(BF)
    dq = jnp.concatenate([turned[1], turned[3]], axis=0) * HD ** (-0.5)
    dq_ref[...] = turn_back(dq, cos_ref[tile], sin_ref[tile]).T.astype(BF)

    @pl.when(tile == tiles - 1)
    def _():
        dv_ref[...] = dv_sum_ref[...].astype(BF)

        def finish(block, _):
            g = dk_sum_ref[rows_of(block), :].T
            dk_ref[rows_of(block), :] = turn_back(g, cos_ref[block], sin_ref[block]).T.astype(BF)
            return 0

        lax.fori_loop(0, total_tiles, finish, 0)


def attend_call(begin, qkv, grad_att, doc, cosine, sine_part):
    tokens = qkv.shape[0]
    width = qkv.shape[1] // 3
    pairs = width // PAIR
    tiles = tokens // TILE
    reach = SPAN + TILE
    query = pl.BlockSpec((TILE, PAIR), lambda p, i, *_: (i, p))
    whole = pl.BlockSpec((tokens, PAIR), lambda p, i, *_: (0, p))
    table = pl.BlockSpec((tiles, ROT // 2, TILE), lambda p, i, *_: (0, 0, 0))
    return pl.pallas_call(
        attend_kernel,
        grid_spec=pltpu.PrefetchScalarGridSpec(
            num_scalar_prefetch=1,
            grid=(pairs, tiles),
            in_specs=[
                query,
                pl.BlockSpec((tokens, PAIR), lambda p, i, *_: (0, pairs + p)),
                pl.BlockSpec((tokens, PAIR), lambda p, i, *_: (0, 2 * pairs + p)),
                query,
                pl.BlockSpec((1, 1, TILE), lambda p, i, *_: (i, 0, 0)),
                table,
                table,
            ],
            out_specs=[query, query, whole, whole],
            scratch_shapes=[
                pltpu.VMEM((2, reach, TILE), F32),
                pltpu.VMEM((2, reach, TILE), F32),
                pltpu.VMEM((tiles, PAIR, TILE), BF),
                pltpu.VMEM((tiles, PAIR, TILE), BF),
                pltpu.VMEM((tokens, PAIR), F32),
                pltpu.VMEM((tokens, PAIR), F32),
            ],
        ),
        out_shape=[jax.ShapeDtypeStruct((tokens, width), BF)] * 4,
        compiler_params=params("arbitrary", "arbitrary"),
        cost_estimate=cost(
            tokens * 800 * width * 4 * 12, tokens * width * 16, tokens * 600 * (width // HD)
        ),
        name="attend",
    )(begin, qkv, qkv, qkv, grad_att, doc, cosine, sine_part)


def normal(v):
    bell = jnp.exp(-0.5 * v * v)
    t = 1.0 / (1.0 + 0.2316418882 * jnp.abs(v))
    tail = 0.7107068705 + t * (-0.7265760135 + t * 0.5307027145)
    tail = 0.127414796 + t * (-0.142248368 + t * tail)
    tail = jnp.where(v < 0, 1.0, -1.0) * (t * tail * bell)
    return jnp.where(v < 0, 0.0, 1.0) + tail, bell * 0.3989422804014327


def units_kernel(two_ref, dy_ref, win_ref, wout_ref, bias_ref, act_ref, pre_ref, sum_ref):
    sides, _, rows, wide = win_ref.shape
    pre = bias_ref[...]
    upstream = 0.0
    for f in range(sides):
        pre = pre + nt(two_ref[:, columns(f, wide)], block_of(win_ref, f, 0, rows))
        upstream = upstream + nt(dy_ref[:, columns(f, wide)], block_of(wout_ref, f, 0, rows))
    cdf, density = normal(pre)
    act_ref[...] = (pre * cdf).astype(BF)
    back = (upstream * (cdf + pre * density)).astype(BF)
    pre_ref[...] = back

    @pl.when(pl.program_id(1) == 0)
    def _():
        sum_ref[...] = jnp.zeros_like(sum_ref)

    sum_ref[...] += jnp.sum(back.astype(F32), axis=0, keepdims=True)


def units_call(two, dy, w, bias, rows):
    tokens, feats = two.shape
    sides, groups, _, wide = w.shape
    units = groups * rows
    taken = max(1, 512 // rows)
    step = taken * rows
    row = pl.BlockSpec((WIDE, feats), lambda j, i: (i, 0))
    line = pl.BlockSpec((1, step), lambda j, i: (0, j))
    out = pl.BlockSpec((WIDE, step), lambda j, i: (i, j))
    return pl.pallas_call(
        units_kernel,
        grid=(units // step, tokens // WIDE),
        in_specs=[
            row,
            row,
            pl.BlockSpec((sides, taken, rows, wide), lambda j, i: (0, j, 0, 0)),
            pl.BlockSpec((sides, taken, rows, wide), lambda j, i: (0, j, 1, 0)),
            line,
        ],
        out_specs=[out, out, line],
        out_shape=[
            jax.ShapeDtypeStruct((tokens, units), BF),
            jax.ShapeDtypeStruct((tokens, units), BF),
            jax.ShapeDtypeStruct((1, units), F32),
        ],
        compiler_params=params("arbitrary", "arbitrary"),
        cost_estimate=cost(10 * tokens * feats * units, 40 * tokens * feats, 2 * tokens * units),
        name="units",
    )(two, dy, w, w, bias)


def unit_grads_kernel(pre_ref, two_ref, act_ref, dy_ref, out_ref):
    _, taken, rows, wide = out_ref.shape
    rows = rows // 2
    got = tn(pre_ref[...], two_ref[...]).astype(BF)
    out_ref[0, :, :rows, :] = got.reshape(taken, rows, wide)
    got = tn(act_ref[...], dy_ref[...]).astype(BF)
    out_ref[0, :, rows:, :] = got.reshape(taken, rows, wide)


def unit_grads_call(pre, two, act, dy, sides, groups):
    tokens, feats = two.shape
    units = act.shape[1]
    rows, wide = units // groups, feats // sides
    taken = max(1, 512 // rows)
    left = pl.BlockSpec((tokens, taken * rows), lambda f, t: (0, t))
    right = pl.BlockSpec((tokens, wide), lambda f, t: (0, f))
    return pl.pallas_call(
        unit_grads_kernel,
        grid=(sides, groups // taken),
        in_specs=[left, right, left, right],
        out_specs=pl.BlockSpec((1, taken, 2 * rows, wide), lambda f, t: (f, t, 0, 0)),
        out_shape=jax.ShapeDtypeStruct((sides, groups, 2 * rows, wide), BF),
        compiler_params=params("arbitrary", "arbitrary"),
        cost_estimate=cost(6 * tokens * feats * units, 4 * tokens * (feats + 2 * units)),
        name="unit_grads",
    )(pre, two, act, dy)


def head_grads_kernel(dq_ref, dk_ref, dv_ref, att_ref, one_ref, dy_ref, after_ref, out_ref):
    groups, _, wide = out_ref.shape[1:]
    pairs = ((dq_ref, one_ref), (dk_ref, one_ref), (dv_ref, one_ref), (att_ref, dy_ref))
    for part, (left, right) in enumerate(pairs):
        got = tn(left[...], right[...]).astype(BF)
        out_ref[0, :, part * HD : (part + 1) * HD, :] = got.reshape(groups, HD, wide)


def head_grads_call(dq, dk, dv, att, one, dy, sides, after):
    tokens, feats = one.shape
    width = dq.shape[1]
    groups, wide = width // HD, feats // sides
    left = pl.BlockSpec((tokens, width), lambda f: (0, 0))
    right = pl.BlockSpec((tokens, wide), lambda f: (0, f))
    return pl.pallas_call(
        head_grads_kernel,
        grid=(sides,),
        in_specs=[left] * 4 + [right] * 2 + [AFTER],
        out_specs=pl.BlockSpec((1, groups, 4 * HD, wide), lambda f: (f, 0, 0, 0)),
        out_shape=jax.ShapeDtypeStruct((sides, groups, 4 * HD, wide), BF),
        compiler_params=params("arbitrary"),
        cost_estimate=cost(12 * tokens * feats * width, 4 * tokens * (feats + 2 * width)),
        name="head_grads",
    )(dq, dk, dv, att, one, dy, after)


def keep_and_send(core_ref, whole, keep_ref, send_ref, place):
    blocks, span, _ = keep_ref.shape
    first = core_ref[0] == 0
    for block in range(blocks):
        at = 2 * block * span
        low, high = whole[at : at + span], whole[at + span : at + 2 * span]
        keep_ref[block, :, place] = jnp.where(first, low, high)
        send_ref[block, :, place] = jnp.where(first, high, low).astype(BF)


def shared_specs(blocks, span, feats):
    block = pl.BlockSpec((WIDE // (2 * span), span, feats), lambda i, *_: (i, 0, 0))
    shape = (blocks, span, feats)
    return [block, block], [jax.ShapeDtypeStruct(shape, F32), jax.ShapeDtypeStruct(shape, BF)]


def output_kernel(core_ref, att_ref, act_ref, wd_ref, wout_ref, keep_ref, send_ref):
    sides, _, rows, wide = wout_ref.shape
    for f in range(sides):
        whole = nn(att_ref[...], block_of(wd_ref, f, 0, HD))
        whole += nn(act_ref[...], block_of(wout_ref, f, 0, rows))
        keep_and_send(core_ref, whole, keep_ref, send_ref, columns(f, wide))


def output_call(core, span, att, act, w_heads, w_units, rows):
    tokens, width = att.shape
    units = act.shape[1]
    sides, groups, _, wide = w_units.shape
    feats = sides * wide
    step = WIDE
    specs, shapes = shared_specs(tokens // (2 * span), span, feats)
    return pl.pallas_call(
        output_kernel,
        grid_spec=pltpu.PrefetchScalarGridSpec(
            num_scalar_prefetch=1,
            grid=(tokens // step,),
            in_specs=[
                pl.BlockSpec((step, width), lambda i, *_: (i, 0)),
                pl.BlockSpec((step, units), lambda i, *_: (i, 0)),
                pl.BlockSpec((sides, groups, HD, wide), lambda i, *_: (0, 0, 3, 0)),
                pl.BlockSpec((sides, groups, rows, wide), lambda i, *_: (0, 0, 1, 0)),
            ],
            out_specs=specs,
        ),
        out_shape=shapes,
        compiler_params=params("arbitrary"),
        cost_estimate=cost(
            3 * tokens * feats * (width + units),
            2 * (tokens * (width + units + 2 * feats) + feats * (width + units)),
        ),
        name="output",
    )(core, att, act, w_heads, w_units)


def back_kernel(
    core_ref,
    dq_ref,
    dk_ref,
    dv_ref,
    pre_ref,
    x_ref,
    w_ref,
    win_ref,
    gain_ref,
    after_ref,
    keep_ref,
    send_ref,
    stat_ref,
    bias_ref,
):
    width = dq_ref.shape[1]
    sides, _, rows, wide = win_ref.shape
    parts = [dq_ref[...], dk_ref[...], dv_ref[...]]
    normed, _ = layer_stats(x_ref[...].astype(F32))

    @pl.when(pl.program_id(0) == 0)
    def _():
        stat_ref[...] = jnp.zeros_like(stat_ref)
        bias_ref[...] = jnp.zeros_like(bias_ref)

    for f in range(sides):
        place = columns(f, wide)
        one = sum(nn(part, block_of(w_ref, f, at * HD, HD)) for at, part in enumerate(parts))
        two = nn(pre_ref[...], block_of(win_ref, f, 0, rows))
        whole = one * gain_ref[0:1, place] + two * gain_ref[1:2, place]
        keep_and_send(core_ref, whole, keep_ref, send_ref, place)
        n = normed[:, place]
        for row, value in enumerate((one * n, two * n, one, two)):
            stat_ref[row : row + 1, place] += jnp.sum(value, axis=0, keepdims=True)
    for row in range(3):
        span = slice(row * width, (row + 1) * width)
        bias_ref[:, span] += jnp.sum(parts[row].astype(F32), axis=0, keepdims=True)


def back_call(core, span, dq, dk, dv, pre, x, w_heads, w_units, gains, rows, after):
    tokens, width = dq.shape
    units = pre.shape[1]
    sides, groups, _, wide = w_units.shape
    feats = sides * wide
    step = WIDE
    part = pl.BlockSpec((step, width), lambda i, *_: (i, 0))
    specs, shapes = shared_specs(tokens // (2 * span), span, feats)
    return pl.pallas_call(
        back_kernel,
        grid_spec=pltpu.PrefetchScalarGridSpec(
            num_scalar_prefetch=1,
            grid=(tokens // step,),
            in_specs=[
                part,
                part,
                part,
                pl.BlockSpec((step, units), lambda i, *_: (i, 0)),
                pl.BlockSpec((step, feats), lambda i, *_: (i, 0)),
                pl.BlockSpec(w_heads.shape, lambda i, *_: (0, 0, 0, 0)),
                pl.BlockSpec((sides, groups, rows, wide), lambda i, *_: (0, 0, 0, 0)),
                pl.BlockSpec((2, feats), lambda i, *_: (0, 0)),
                AFTER,
            ],
            out_specs=specs
            + [
                pl.BlockSpec((4, feats), lambda i, *_: (0, 0)),
                pl.BlockSpec((1, 3 * width), lambda i, *_: (0, 0)),
            ],
        ),
        out_shape=shapes
        + [
            jax.ShapeDtypeStruct((4, feats), F32),
            jax.ShapeDtypeStruct((1, 3 * width), F32),
        ],
        compiler_params=params("arbitrary"),
        cost_estimate=cost(
            3 * tokens * feats * (3 * width + units),
            2 * (tokens * (3 * width + units + 3 * feats) + feats * (3 * width + units)),
        ),
        name="back",
    )(core, dq, dk, dv, pre, x, w_heads, w_units, gains, after)


def fold_kernel(side_ref, own_ref, far_ref, after_ref, out_ref):
    out_ref[...] = (own_ref[0].astype(F32) + far_ref[...].astype(F32)).astype(BF)


def fold_call(side, full, far, after):
    groups, rows, wide = far.shape
    block = pl.BlockSpec((1, rows, wide), lambda i, *_: (i, 0, 0))
    return pl.pallas_call(
        fold_kernel,
        grid_spec=pltpu.PrefetchScalarGridSpec(
            num_scalar_prefetch=1,
            grid=(groups,),
            in_specs=[
                pl.BlockSpec((1, 1, rows, wide), lambda i, side_ref: (side_ref[0], i, 0, 0)),
                block,
                AFTER,
            ],
            out_specs=block,
        ),
        out_shape=jax.ShapeDtypeStruct(far.shape, BF),
        compiler_params=params("arbitrary"),
        cost_estimate=cost(far.size * 2, far.size * 6),
        name="fold",
    )(side, full, far, after)


def finish_kernel(keep_ref, far_ref, x_ref, dy_ref, after_ref, out_ref):
    e = keep_ref[0] + far_ref[0].astype(F32)
    normed, inverse = layer_stats(x_ref[0].astype(F32))
    through = inverse * (
        e
        - jnp.mean(e, axis=-1, keepdims=True)
        - normed * jnp.mean(e * normed, axis=-1, keepdims=True)
    )
    out_ref[0] = (dy_ref[0].astype(F32) + through).astype(BF)


def finish_call(keep, far, x, dy, after):
    block = pl.BlockSpec((1,) + keep.shape[1:], lambda i: (i, 0, 0))
    return pl.pallas_call(
        finish_kernel,
        grid=(keep.shape[0],),
        in_specs=[block] * 4 + [AFTER],
        out_specs=block,
        out_shape=jax.ShapeDtypeStruct(keep.shape, BF),
        compiler_params=params("arbitrary"),
        cost_estimate=cost(keep.size * 20, keep.size * 12),
        name="finish",
    )(keep, far, x, dy, after)


def swap_cores(v):
    return lax.ppermute(v, "ctx", [(0, 1), (1, 0)])


def body(
    hidden_in,
    segment_ids,
    norm_gains,
    norm_biases,
    qkv_weight,
    qkv_bias,
    dense_weight,
    fc_in_weight,
    fc_in_bias,
    fc_out_weight,
    out_biases,
    out_grad,
):
    chips = lax.axis_size("tensor")
    rows_of_chips = lax.axis_size("fsdp")
    tensor_index = lax.axis_index("tensor")
    core = lax.axis_index("ctx")
    side = lax.axis_index("fsdp")
    local_seqs, span, feats = hidden_in.shape
    sharing = chips // local_seqs
    ranks = 2 * sharing
    tokens = 2 * chips * span
    tiles = tokens // TILE
    local_heads = qkv_bias.shape[0]
    local_units = fc_in_bias.shape[0]
    cols = qkv_weight.shape[0]
    own_seq = tensor_index // sharing
    rank = (tensor_index % sharing) * 2 + core
    swap = (
        sharing == 1 and local_heads == 2 and rows_of_chips == 2 and chips & (chips - 1) == 0
    )
    heads = chips * local_heads // ranks
    units = chips * local_units // ranks
    gains = norm_gains.astype(F32)
    shifts = norm_biases.astype(F32)
    core_scalar = core.reshape(1)

    def to_chip(rows):
        if sharing > 1:
            rows = jnp.repeat(rows, sharing, axis=0)
        return lax.all_to_all(rows, "tensor", 0, 0, tiled=True)

    def from_chip(rows):
        rows = lax.all_to_all(rows, "tensor", 0, 0, tiled=True)
        if sharing > 1:
            rows = rows.reshape(local_seqs, sharing, span, feats).astype(F32)
            rows = jnp.sum(rows, axis=1).astype(BF)
        return rows

    def ordered(own, far, axis):
        return jnp.where(
            core == 0,
            jnp.concatenate([own, far], axis=axis),
            jnp.concatenate([far, own], axis=axis),
        )

    def gather_rows(shard, extra=None):
        rows = shard.shape[1]
        if swap:
            own = lax.dynamic_index_in_dim(shard, core, 0, keepdims=False)
            far = lax.dynamic_index_in_dim(shard, 1 - core, 0, keepdims=False)
            mine = ordered(own, swap_cores(far), 1)
            if extra is not None:
                mine = jnp.concatenate([mine, extra])
            full = lax.all_gather(mine, CHIPS, axis=0, tiled=False)
            return full.reshape((rows_of_chips, chips) + mine.shape)
        full = lax.all_gather(shard.reshape(pieces * rows, cols), EVERY, axis=0, tiled=False)
        full = full.reshape(rows_of_chips, chips, 2, pieces, rows, cols)
        full = full.transpose(1, 3, 4, 0, 2, 5).reshape(1, chips * pieces, rows, feats)
        count = chips * pieces // ranks
        return lax.dynamic_slice_in_dim(full, rank * count, count, 1)

    def side_swap(v):
        return lax.ppermute(v, "fsdp", [(0, 1), (1, 0)])

    def sum_chips(full, axes):
        mine = lax.psum_scatter(full, axes, scatter_dimension=0, tiled=True)
        return with_layout_constraint(mine, Layout((0, 1, 2)))

    def to_cores(mine):
        mine = mine.reshape(-1, 2, cols)
        own = lax.dynamic_index_in_dim(mine, core, 1, keepdims=False)
        far = lax.dynamic_index_in_dim(mine, 1 - core, 1, keepdims=False)
        return ordered(own[None], swap_cores(far)[None], 0).astype(F32)

    def scatter_rows(full):
        rows = full.shape[2]
        wide = jnp.zeros((chips * pieces, rows, feats), BF)
        wide = lax.dynamic_update_slice_in_dim(wide, full[0], rank * full.shape[1], 0)
        wide = wide.reshape(chips, pieces, rows, rows_of_chips, 2, cols)
        wide = wide.transpose(3, 0, 4, 1, 2, 5).reshape(-1, pieces * rows, cols)
        mine = lax.psum_scatter(wide, EVERY, scatter_dimension=0, tiled=True)
        return mine.reshape(pieces, rows, cols).astype(F32)

    def own_pieces(full):
        full = full.reshape((chips * pieces,) + full.shape[2:])
        count = chips * pieces // ranks
        return lax.dynamic_slice_in_dim(full, rank * count, count, 0)

    def place_pieces(part):
        size = part.shape[1]
        if swap:
            wide = jnp.zeros((chips, pieces, size), F32)
            return lax.dynamic_update_slice_in_dim(wide, part[:, None], core, 1)
        wide = jnp.zeros((chips * pieces, size), F32)
        wide = lax.dynamic_update_slice_in_dim(wide, part, rank * part.shape[0], 0)
        return wide.reshape(chips, pieces, size)

    pieces = local_heads
    unit_rows = local_units // pieces
    unit_shards = jnp.concatenate(
        [
            fc_in_weight.T.reshape(pieces, unit_rows, cols),
            fc_out_weight.reshape(pieces, unit_rows, cols),
        ],
        axis=1,
    )
    head_shards = jnp.concatenate([qkv_weight.transpose(1, 2, 0), dense_weight], axis=1)

    own_x = to_chip(hidden_in)
    own_dy = to_chip(out_grad)
    if swap:
        shift_row = jnp.concatenate(
            [
                lax.dynamic_index_in_dim(qkv_bias, core, 0, keepdims=False),
                lax.dynamic_slice_in_dim(fc_in_bias, core * unit_rows, unit_rows, 0),
            ]
        )
        shift_rows = jnp.zeros((16, 2 * cols), BF)
        shift_rows = lax.dynamic_update_slice(shift_rows, shift_row[None], (0, 0))
        w_units = gather_rows(unit_shards, shift_rows)
        bias_all = w_units[0, :, 2 * unit_rows, :].astype(F32)
        w_heads = gather_rows(head_shards)
        qkv_shift = bias_all[:, : 3 * HD]
        unit_shift = bias_all[:, 3 * HD : 3 * HD + unit_rows]
    else:
        bias_vector = jnp.concatenate([qkv_bias.reshape(-1), fc_in_bias]).astype(F32)
        bias_all = lax.all_gather(bias_vector, "tensor", axis=0, tiled=False)
        qkv_size = local_heads * 3 * HD
        qkv_shift = own_pieces(bias_all[:, :qkv_size].reshape(chips, pieces, 3 * HD))
        unit_shift = own_pieces(bias_all[:, qkv_size:].reshape(chips, pieces, unit_rows))
        w_units = gather_rows(unit_shards)
        w_heads = gather_rows(head_shards)
    qkv_shift = qkv_shift.reshape(heads, 3, HD).transpose(1, 0, 2).reshape(1, -1)
    unit_shift = unit_shift.reshape(1, units)
    sides, groups = w_units.shape[:2]

    segments = lax.dynamic_index_in_dim(segment_ids, own_seq, 0, keepdims=False)
    places = lax.broadcasted_iota(jnp.int32, (tokens,), 0)
    change = jnp.concatenate(
        [jnp.ones((1,), jnp.int32), (segments[1:] != segments[:-1]).astype(jnp.int32)]
    )
    starts = lax.cummax(places * change, axis=0)
    begin = starts[::TILE] // TILE
    freqs = 10000.0 ** (-jnp.arange(0, ROT, 2, dtype=F32) / ROT)
    relative = (places - starts).astype(F32)[:, None]
    lane = jnp.arange(PAIR) % HD
    turning = lane < ROT
    lane_freqs = jnp.where(turning, freqs[lane % (ROT // 2)], 0.0)
    angle = relative * lane_freqs
    cos_lanes = jnp.cos(angle)
    sin_lanes = jnp.sin(angle) * jnp.where(lane < ROT // 2, -1.0, 1.0)
    cos_rows = cos_lanes[:, : ROT // 2].reshape(tiles, TILE, ROT // 2).transpose(0, 2, 1)
    sin_rows = -sin_lanes[:, : ROT // 2].reshape(tiles, TILE, ROT // 2).transpose(0, 2, 1)

    doc = starts.reshape(tiles, 1, TILE)
    x, one, two = merge_call(core_scalar, own_x, swap_cores(own_x), None, gains, shifts)
    (dy,) = merge_call(core_scalar, own_dy, swap_cores(own_dy), one)
    active, grad_pre, unit_sum = units_call(two, dy, w_units, unit_shift, unit_rows)
    unit_grads = unit_grads_call(grad_pre, two, active, dy, sides, groups)
    if swap:
        unit_sums = sum_chips(unit_grads.reshape((-1,) + unit_grads.shape[2:]), CHIPS)
        grad_units = to_cores(unit_sums)
    else:
        grad_units = scatter_rows(unit_grads)
    qkv, grad_att = qkv_call(one, dy, w_heads, qkv_shift, cos_lanes, sin_lanes, unit_grads)
    attended, dq, dk, dv = attend_call(begin, qkv, grad_att, doc, cos_rows, sin_rows)
    out_keep, out_send = output_call(core_scalar, span, attended, active, w_heads, w_units, unit_rows)

    bias_rows = out_biases.astype(F32)
    wide_x = own_x.astype(F32)
    residual = wide_x + bias_rows[0] + bias_rows[1]
    upstream = own_dy
    if sharing > 1:
        leader = tensor_index % sharing == 0
        residual = jnp.where(leader, residual, 0.0)
        upstream = jnp.where(leader, upstream, 0.0).astype(BF)
    out_part = out_keep + swap_cores(out_send).astype(F32)
    out_low = (residual + out_part).astype(BF)
    hidden_out = from_chip(out_low)

    head_grads = head_grads_call(dq, dk, dv, attended, one, dy, sides, out_low)
    e_keep, e_send, stats, qkv_sum = back_call(
        core_scalar, span, dq, dk, dv, grad_pre, x, w_heads, w_units, gains, unit_rows, head_grads
    )
    if swap:
        far = lax.dynamic_index_in_dim(head_grads, 1 - side, 0, keepdims=False)
        folded = fold_call(side.reshape(1), head_grads, side_swap(far), unit_sums)
        grad_heads = to_cores(sum_chips(folded, "tensor"))
    else:
        grad_heads = scatter_rows(head_grads)
    input_rows = finish_call(e_keep, swap_cores(e_send), own_x, upstream, hidden_out)
    input_grad = from_chip(input_rows)

    qkv_sum = qkv_sum.reshape(3, heads, HD).transpose(1, 0, 2).reshape(-1, 3 * HD)
    qkv_sum = place_pieces(qkv_sum)
    unit_sum = place_pieces(unit_sum.reshape(-1, unit_rows))
    out_sum = jnp.sum(out_grad.astype(F32), axis=(0, 1))
    packed = jnp.concatenate(
        [stats.reshape(-1), out_sum, qkv_sum.reshape(-1), unit_sum.reshape(-1)]
    )
    if swap:
        packed = packed + swap_cores(packed)
        packed = packed + side_swap(packed)
        bit = 1
        while bit < chips:
            packed = packed + lax.ppermute(packed, "tensor", [(i, i ^ bit) for i in range(chips)])
            bit *= 2
    else:
        packed = lax.psum(packed, EVERY)
    sums = packed[: 5 * feats].reshape(5, feats)
    qkv_size = chips * local_heads * 3 * HD
    qkv_all = packed[5 * feats : 5 * feats + qkv_size].reshape(chips, local_heads, 3 * HD)
    unit_all = packed[5 * feats + qkv_size :].reshape(chips, local_units)
    grad_qkv_b = lax.dynamic_index_in_dim(qkv_all, tensor_index, 0, keepdims=False)
    grad_unit_b = lax.dynamic_index_in_dim(unit_all, tensor_index, 0, keepdims=False)
    return (
        hidden_out,
        input_grad,
        sums[0:2],
        sums[2:4],
        grad_heads[:, : 3 * HD].transpose(2, 0, 1),
        grad_qkv_b,
        grad_heads[:, 3 * HD :],
        grad_units[:, :unit_rows].reshape(local_units, cols).T,
        grad_unit_b,
        grad_units[:, unit_rows:].reshape(local_units, cols),
        jnp.stack([sums[4], sums[4]]),
    )


def solution(mesh):
    rows = P("fsdp", ("tensor", "ctx"), None)
    weights = (
        P(("fsdp", "ctx"), "tensor", None),
        P("tensor", None),
        P("tensor", None, ("fsdp", "ctx")),
        P(("fsdp", "ctx"), "tensor"),
        P("tensor"),
        P("tensor", ("fsdp", "ctx")),
    )
    return jax.shard_map(
        body,
        mesh=mesh,
        in_specs=(rows, P("fsdp", None), P(), P()) + weights + (P(), rows),
        out_specs=(rows, rows, P(), P()) + weights + (P(),),
        check_vma=False,
    )
```

time: 852 us -> 629 us (0.74)
  blocking collectives: 284 us -> 90.4 us
  local copies, waits for them, and re-layouts: 124 us -> 23.7 us
  Pallas kernels: 186 us -> 245 us
  waiting for transfers between devices: 144 us -> 193 us
  matrix products: 44.1 us -> 0 us
  starting transfers between devices: 13.2 us -> 36.4 us
    ppermute x4 -> x14, waiting for transfers between devices: 0.01 us -> 85.6 us  [the longest x3 44.3 us: body(): lax.ppermute(packed, 'tensor', [(i, i ^ bit) for i in range(chips)])]
    psum x1 -> x0, blocking collectives: 85.1 us -> none  [body(): packed = lax.psum(packed, EVERY)]
    all_to_all x9 -> x1, blocking collectives: 168 us -> 90.4 us  [to_chip(): return lax.all_to_all(rows, 'tensor', 0, 0, tiled=True)]
    reduce_scatter x4 -> x2, waiting for transfers between devices: 89.8 us -> 14 us  [sum_chips(): mine = lax.psum_scatter(full, axes, scatter_dimension=0, tiled=True)]
    pallas_call x5 -> x10, Pallas kernels: 106 us -> 163 us  [the longest x1 34.7 us: units_call(): pl.pallas_call(units_kernel, grid=(units // step, tokens // WIDE), in_spe...]
    dot_general x7 -> x0, matrix products: 44.1 us -> none  [the longest x6 40.4 us: tn(): lax.dot_general(a, b, (((0,), (0,)), ((), ())), preferred_element_type=F32)]
    all_to_all x3, waiting for transfers between devices: 54.5 us -> 93.6 us  [the longest x1 93.6 us: to_chip(): return lax.all_to_all(rows, 'tensor', 0, 0, tiled=True)]
    all_gather x1 -> x0, blocking collectives: 30.6 us -> none  [body(): bias_all = lax.all_gather(bias_vector, 'tensor', axis=0, tiled=False)]
  transfers between devices with their start and end apart: 15 -> 21, of which waited for: 3 -> 11; matrix products, arithmetic and copies ran while one was open for 23% -> 6% of each run, Pallas kernels for 22% -> 39%
where the time goes in v2:
time: 629 us; the launch traced here: 626 us
  Pallas kernels  245 us (39%)
  waiting for transfers between devices  193 us (31%)
  blocking collectives  90.4 us (14%)
  starting transfers between devices  36.4 us (6%)
  local copies, waits for them, and re-layouts  23.7 us (4%)
  other arithmetic  23.3 us (4%)
  between operations  14.2 us (2%)
    all_to_all x1, waiting for transfers between devices, to_chip(): return lax.all_to_all(rows, 'tensor', 0, 0, tiled=True)  93.6 us
    all_to_all x1, blocking collectives, to_chip(): return lax.all_to_all(rows, 'tensor', 0, 0, tiled=True)  90.4 us
    pallas_call x1, Pallas kernels, attend_call(): pl.pallas_call(attend_kernel, grid_spec=pltpu.PrefetchScalarGridSpec(num_...  82 us
    ppermute x3, waiting for transfers between devices, body(): lax.ppermute(packed, 'tensor', [(i, i ^ bit) for i in range(chips)])  44.3 us
    pallas_call x1, Pallas kernels, units_call(): pl.pallas_call(units_kernel, grid=(units // step, tokens // WIDE), in_spe...  34.7 us
    ppermute x2, waiting for transfers between devices, side_swap(): return lax.ppermute(v, 'fsdp', [(0, 1), (1, 0)])  32.3 us
    pallas_call x1, Pallas kernels, back_call(): pl.pallas_call(back_kernel, grid_spec=pltpu.PrefetchScalarGridSpec(num_sc...  26.4 us
    pallas_call x1, Pallas kernels, unit_grads_call(): pl.pallas_call(unit_grads_kernel, grid=(sides, groups // taken), in_specs...  25.9 us
  transfers between devices with their start and end apart: 21, of which 11 were waited for; matrix products, arithmetic and copies ran while one was open for 6% of the time, Pallas kernels for 39%

profile of v2, /device:TPU:0, one launch (start us, length us, event | category | flops | bytes accessed | tf_op | source)
XLA Modules:
  0.0 626.5 jit_solution(2258570438921789912)
XLA Ops:
  12.0 90.4 %all_to_all.20.own_ref.x_ref = bf16[8,128,1024]{2,1,0:T(8,128)(2,1)S(1)} all-to-all(bf16[8,128,1024]{2,1,0:T(8,128)(2,1)} %param.12), channel_id=1, replica_groups=mesh['fsdp'=2,'tensor'=8,'ctx'=2] {'tensor'}, dimensions={0} | all-to-all | bytes 4194304 | tf_op jit(solution)/shard_map/all_to_all | solution.py:687
  102.5 4.5 all-to-all-start.1
  107.1 93.6 %all-to-all-done.1.own_ref.dy_ref = bf16[8,128,1024]{2,1,0:T(8,128)(2,1)} async-done(((bf16[8,128,1024]{2,1,0:T(8,128)(2,1)}), bf16[8,128,1024]{2,1,0:T(8,128)(2,1)}, u32[]{:S(2)}, u32[]{:S(2)}) %all-to-all-start.1) | async-done | bytes 2097184 | tf_op jit(solution)/shard_map/all_to_all | solution.py:687
  206.8 9.1 %norms.1 = (bf16[2048,1024]{1,0:T(8,128)(2,1)}, bf16[2048,1024]{1,0:T(8,128)(2,1)}, bf16[2048,1024]{1,0:T(8,128)(2,1)}) custom-call(s32[1]{0:T(128)} %bitcast.2.core_ref, bf16[8,128,1024]{2,1,0:T(8,128)(2,1)} %copy-done.2, bf16[8,128,1024]{2,1,0:T(8,128)(2,1)} %collective-permute-done.far_ref, f32[2,1024]{1,0:T(2,128)} %convert_element_type.47.gain_ref, ...), custom_call_target="tpu_custom_call" | custom-call | flops 25165824 | bytes 16777216 | tf_op jit(solution)/shard_map/norms/pallas_call | solution.py:83
  215.9 6.6 %merge.1.dy_ref = bf16[2048,1024]{1,0:T(8,128)(2,1)} custom-call(s32[1]{0:T(128)} %bitcast.2.core_ref, bf16[8,128,1024]{2,1,0:T(8,128)(2,1)} %all-to-all-done.1.own_ref.dy_ref, bf16[8,128,1024]{2,1,0:T(8,128)(2,1)} %collective-permute-done.1.far_ref, bf16[2048,1024]{1,0:T(8,128)(2,1)} %get-tuple-element.29.after_ref.one_ref), custom_call_target="tpu_custom_call" | custom-call | flops 25165824 | bytes 8388608 | tf_op jit(solution)/shard_map/merge/pallas_call | solution.py:83
  224.1 34.7 %units.1 = (bf16[2048,2048]{1,0:T(8,128)(2,1)}, bf16[2048,2048]{1,0:T(8,128)(2,1)}, f32[1,2048]{1,0:T(1,128)}) custom-call(bf16[2048,1024]{1,0:T(8,128)(2,1)} %get-tuple-element.30.two_ref, bf16[2048,1024]{1,0:T(8,128)(2,1)} %merge.1.dy_ref, bf16[2,8,528,512]{3,2,1,0:T(8,128)(2,1)} %bitcast.132, bf16[2,8,528,512]{3,2,1,0:T(8,128)(2,1)} %bitcast.133, ...), custom_call_target="tpu_custom_call" | custom-call | flops 42949672960 | bytes 83886080 | tf_op jit(solution)/shard_map/units/pallas_call | solution.py:377
  258.7 25.9 %unit_grads.1.after_ref = bf16[2,8,512,512]{3,2,1,0:T(8,128)(2,1)} custom-call(bf16[2048,2048]{1,0:T(8,128)(2,1)} %get-tuple-element.31.pre_ref, bf16[2048,1024]{1,0:T(8,128)(2,1)} %get-tuple-element.30.two_ref, bf16[2048,2048]{1,0:T(8,128)(2,1)} %get-tuple-element.32.act_ref, bf16[2048,1024]{1,0:T(8,128)(2,1)} %merge.1.dy_ref), custom_call_target="tpu_custom_call" | custom-call | flops 25769803776 | bytes 41943040 | tf_op jit(solution)/shard_map/unit_grads/pallas_call | solution.py:415
  287.1 5.2 compare_select_fusion.9
  300.5 14.2 %qkv.1 = (bf16[2048,1536]{1,0:T(8,128)(2,1)}, bf16[2048,512]{1,0:T(8,128)(2,1)}) custom-call(bf16[2048,1024]{1,0:T(8,128)(2,1)} %get-tuple-element.29.after_ref.one_ref, bf16[2048,1024]{1,0:T(8,128)(2,1)} %merge.1.dy_ref, bf16[2,8,256,512]{3,2,1,0:T(8,128)(2,1)} %bitcast.136, f32[1,1536]{1,0:T(1,128)} %reshape.328.bias_ref, f32[2048,128]{1,0:T(8,128)} %copy-done.8, ...), custom_call_target="tpu_custom_call" | custom-call | flops 17179869184 | bytes 25165824 | tf_op jit(solution)/shard_map/qkv/pallas_call | solution.py:143
  314.6 82.0 %attend.1 = (bf16[2048,512]{1,0:T(8,128)(2,1)}, bf16[2048,512]{1,0:T(8,128)(2,1)}, bf16[2048,512]{1,0:T(8,128)(2,1)}, bf16[2048,512]{1,0:T(8,128)(2,1)}) custom-call(s32[8]{0:T(128)} %and_select_fusion.3.begin_ref, bf16[2048,1536]{1,0:T(8,128)(2,1)} %get-tuple-element.33.q_ref.k_ref.v_ref, bf16[2048,1536]{1,0:T(8,128)(2,1)} %get-tuple-element.33.q_ref.k_ref.v_ref, ...), custom_call_target="tpu_custom_call" | custom-call | flops 40265318400 | bytes 16777216 | tf_op jit(solution)/shard_map/attend/pallas_call | solution.py:307
  396.6 16.3 %output.1 = (f32[8,128,1024]{2,1,0:T(8,128)}, bf16[8,128,1024]{2,1,0:T(8,128)(2,1)}) custom-call(s32[1]{0:T(128)} %bitcast.2.core_ref, bf16[2048,512]{1,0:T(8,128)(2,1)} %get-tuple-element.35.att_ref, bf16[2048,2048]{1,0:T(8,128)(2,1)} %get-tuple-element.32.act_ref, bf16[2,8,256,512]{3,2,1,0:T(8,128)(2,1)} %bitcast.137, bf16[2,8,528,512]{3,2,1,0:T(8,128)(2,1)} %bitcast.134), custom_call_target="tpu_custom_call" | custom-call | flops 16106127360 | bytes 24117248 | tf_op jit(solution)/shard_map/output/pallas_call | solution.py:484
  413.2 4.2 collective-permute-done.4
  417.4 5.5 add_convert_fusion.after_ref
  422.9 18.9 %all-to-all-start.2 = ((bf16[8,128,1024]{2,1,0:T(8,128)(2,1)}), bf16[8,128,1024]{2,1,0:T(8,128)(2,1)S(1)}, u32[]{:S(2)}, u32[]{:S(2)}) async-start(bf16[8,128,1024]{2,1,0:T(8,128)(2,1)} %add_convert_fusion.after_ref), calls=%async_computation.2 | async-start | bytes 4194304 | tf_op jit(solution)/shard_map/all_to_all | solution.py:690
  441.8 15.2 %head_grads.1.after_ref.own_ref = bf16[2,8,256,512]{3,2,1,0:T(8,128)(2,1)} custom-call(bf16[2048,512]{1,0:T(8,128)(2,1)} %get-tuple-element.38.dq_ref, bf16[2048,512]{1,0:T(8,128)(2,1)} %get-tuple-element.39.dk_ref, bf16[2048,512]{1,0:T(8,128)(2,1)} %get-tuple-element.40.dv_ref, bf16[2048,512]{1,0:T(8,128)(2,1)} %get-tuple-element.35.att_ref, ...), custom_call_target="tpu_custom_call" | custom-call | flops 12884901888 | bytes 16777216 | tf_op jit(solution)/shard_map/head_grads/pallas_call | solution.py:441
  458.9 26.4 %back.1 = (f32[8,128,1024]{2,1,0:T(8,128)}, bf16[8,128,1024]{2,1,0:T(8,128)(2,1)}, f32[4,1024]{1,0:T(4,128)}, f32[1,1536]{1,0:T(1,128)}) custom-call(s32[1]{0:T(128)} %bitcast.2.core_ref, bf16[2048,512]{1,0:T(8,128)(2,1)} %get-tuple-element.38.dq_ref, bf16[2048,512]{1,0:T(8,128)(2,1)} %get-tuple-element.39.dk_ref, ...), custom_call_target="tpu_custom_call" | custom-call | flops 22548578304 | bytes 34603008 | tf_op jit(solution)/shard_map/back/pallas_call | solution.py:555
  485.4 28.2 %collective-permute-done.11.far_ref = bf16[8,256,512]{2,1,0:T(8,128)(2,1)} collective-permute-done((bf16[8,256,512]{2,1,0:T(8,128)(2,1)S(1)}, bf16[8,256,512]{2,1,0:T(8,128)(2,1)}, u32[]{:S(2)}, u32[]{:S(2)}) %collective-permute-start.11) | collective-permute-done | bytes 2097184 | tf_op jit(solution)/shard_map/ppermute | solution.py:720
  513.6 6.2 fold.1
  521.2 8.6 %finish.1 = bf16[8,128,1024]{2,1,0:T(8,128)(2,1)} custom-call(f32[8,128,1024]{2,1,0:T(8,128)} %get-tuple-element.42.keep_ref, bf16[8,128,1024]{2,1,0:T(8,128)(2,1)} %collective-permute-done.5.far_ref, bf16[8,128,1024]{2,1,0:T(8,128)(2,1)} %copy-done.2, bf16[8,128,1024]{2,1,0:T(8,128)(2,1)} %all-to-all-done.1.own_ref.dy_ref, bf16[8,128,1024]{2,1,0:T(8,128)(2,1)} %copy-done.4), custom_call_target="tpu_custom_call" | custom-call | flops 20971520 | bytes 12582912 | tf_op jit(solution)/shard_map/finish/pallas_call | solution.py:630
  529.8 4.5 all-to-all-start.3
  543.0 12.7 %collective-permute-done.8 = f32[12288]{0:T(1024)S(1)} collective-permute-done((f32[12288]{0:T(1024)S(1)}, f32[12288]{0:T(1024)S(1)}, u32[]{:S(2)}, u32[]{:S(2)}) %collective-permute-start.8) | collective-permute-done | bytes 49184 | tf_op jit(solution)/shard_map/ppermute | solution.py:863
  556.9 20.7 %collective-permute-done.9 = f32[12288]{0:T(1024)S(1)} collective-permute-done((f32[12288]{0:T(1024)S(1)}, f32[12288]{0:T(1024)S(1)}, u32[]{:S(2)}, u32[]{:S(2)}) %collective-permute-start.9) | collective-permute-done | bytes 49184 | tf_op jit(solution)/shard_map/ppermute | solution.py:863
  580.9 10.9 %collective-permute-done.10 = f32[12288]{0:T(1024)S(1)} collective-permute-done((f32[12288]{0:T(1024)S(1)}, f32[12288]{0:T(1024)S(1)}, u32[]{:S(2)}, u32[]{:S(2)}) %collective-permute-start.10) | collective-permute-done | bytes 49184 | tf_op jit(solution)/shard_map/ppermute | solution.py:863
  596.5 14.0 %reduce-scatter.5.cloned.1.call-done = bf16[1,256,512]{2,1,0:T(8,128)(2,1)} async-done(((bf16[8,256,512]{2,1,0:T(8,128)(2,1)}), bf16[1,256,512]{2,1,0:T(8,128)(2,1)}) %reduce-scatter.5.cloned.1.call-update) | async-done | bytes 262160 | tf_op jit(solution)/shard_map/reduce_scatter | solution.py:723
  (157 shorter events, 53.9 us)
Async XLA Ops:
  7.2 215.3 %all-gather.6.cloned.1.call-start = ((), (), s32[]{:S(2)}) async-start(), calls=%async_computation.9 | async-start | bytes 9191424 | tf_op jit(solution)/shard_map/all_gather | solution.py:711
  9.3 1.7 collective-permute-start.3
  102.5 98.3 %copy-start.11 = (bf16[2,64,256]{2,1,0:T(8,128)(2,1)S(1)}, bf16[2,64,256]{2,1,0:T(8,128)(2,1)}, u32[]{:S(2)}) copy-start(bf16[2,64,256]{2,1,0:T(8,128)(2,1)} %param.18) | copy-start | bytes 196612
  102.5 103.1 %copy-start.16 = (bf16[2,1024]{1,0:T(2,128)(2,1)S(1)}, bf16[2,1024]{1,0:T(2,128)(2,1)}, u32[]{:S(2)}) copy-start(bf16[2,1024]{1,0:T(2,128)(2,1)} %param.14) | copy-start | bytes 12292
  102.5 103.7 %copy-start.17 = (bf16[2,1024]{1,0:T(2,128)(2,1)S(1)}, bf16[2,1024]{1,0:T(2,128)(2,1)}, u32[]{:S(2)}) copy-start(bf16[2,1024]{1,0:T(2,128)(2,1)} %param.15) | copy-start | bytes 12292
  102.5 98.2 %all-to-all-start.1 = ((bf16[8,128,1024]{2,1,0:T(8,128)(2,1)}), bf16[8,128,1024]{2,1,0:T(8,128)(2,1)}, u32[]{:S(2)}, u32[]{:S(2)}) async-start(bf16[8,128,1024]{2,1,0:T(8,128)(2,1)} %param.23), calls=%async_computation.1 | async-start | bytes 4194304 | tf_op jit(solution)/shard_map/all_to_all | solution.py:687
  107.0 193.5 %all-gather.4.cloned.1.call-start = ((), (), s32[]{:S(2)}) async-start(), calls=%async_computation.6 | async-start | bytes 4456448 | tf_op jit(solution)/shard_map/all_gather | solution.py:711
  107.0 99.8 %collective-permute-start = (bf16[8,128,1024]{2,1,0:T(8,128)(2,1)S(1)}, bf16[8,128,1024]{2,1,0:T(8,128)(2,1)}, u32[]{:S(2)}, u32[]{:S(2)}) collective-permute-start(bf16[8,128,1024]{2,1,0:T(8,128)(2,1)S(1)} %all_to_all.20.own_ref.x_ref), channel_id=1, source_target_pairs={{0,1},{1,0},{2,3},{3,2},{4,5},{5,4},{6,7},{7,6},{8,9},{9,8},{10,11... | collective-permute-start | bytes 6291464 | tf_op jit(solution)/shard_map/ppermute | solution.py:643
  200.7 15.2 %collective-permute-start.1 = (bf16[8,128,1024]{2,1,0:T(8,128)(2,1)}, bf16[8,128,1024]{2,1,0:T(8,128)(2,1)}, u32[]{:S(2)}, u32[]{:S(2)}) collective-permute-start(bf16[8,128,1024]{2,1,0:T(8,128)(2,1)} %all-to-all-done.1.own_ref.dy_ref), channel_id=1, source_target_pairs={{0,1},{1,0},{2,3},{3,2},{4,5},{5,4},{6,7},{7,6},{8,9},{9,8},{10,11... | collective-permute-start | bytes 6291464 | tf_op jit(solution)/shard_map/ppermute | solution.py:643
  200.8 3.9 collective-permute-start.2
  205.5 308.1 %reduce-scatter.3.cloned.1.call-start = ((), (), s32[]{:S(2)}) async-start(), calls=%async_computation.7 | async-start | bytes 8912896 | tf_op jit(solution)/shard_map/reduce_scatter | solution.py:723
  412.9 4.5 collective-permute-start.4
  422.9 96.9 %all-to-all-start.2 = ((bf16[8,128,1024]{2,1,0:T(8,128)(2,1)}), bf16[8,128,1024]{2,1,0:T(8,128)(2,1)S(1)}, u32[]{:S(2)}, u32[]{:S(2)}) async-start(bf16[8,128,1024]{2,1,0:T(8,128)(2,1)} %add_convert_fusion.after_ref), calls=%async_computation.2 | async-start | bytes 4194304 | tf_op jit(solution)/shard_map/all_to_all | solution.py:690
  441.8 168.7 %reduce-scatter.5.cloned.1.call-start = ((), (), s32[]{:S(2)}) async-start(), calls=%async_computation.8 | async-start | bytes 2359296 | tf_op jit(solution)/shard_map/reduce_scatter | solution.py:723
  458.8 54.8 %collective-permute-start.11 = (bf16[8,256,512]{2,1,0:T(8,128)(2,1)S(1)}, bf16[8,256,512]{2,1,0:T(8,128)(2,1)}, u32[]{:S(2)}, u32[]{:S(2)}) collective-permute-start(bf16[8,256,512]{2,1,0:T(8,128)(2,1)S(1)} %dynamic-slice_bitcast_fusion), channel_id=1, source_target_pairs={{0,16},{16,0},{1,17},{17,1},{2,18},{18,2},{3,19},{19,3},{4,20},{20... | collective-permute-start | bytes 6291464 | tf_op jit(solution)/shard_map/ppermute | solution.py:720
  485.3 34.6 %collective-permute-start.5 = (bf16[8,128,1024]{2,1,0:T(8,128)(2,1)}, bf16[8,128,1024]{2,1,0:T(8,128)(2,1)}, u32[]{:S(2)}, u32[]{:S(2)}) collective-permute-start(bf16[8,128,1024]{2,1,0:T(8,128)(2,1)} %get-tuple-element.43), channel_id=1, source_target_pairs={{0,1},{1,0},{2,3},{3,2},{4,5},{5,4},{6,7},{7,6},{8,9},{9,8},{10,11... | collective-permute-start | bytes 6291464 | tf_op jit(solution)/shard_map/ppermute | solution.py:643
  529.8 66.6 %all-to-all-start.3 = ((bf16[8,128,1024]{2,1,0:T(8,128)(2,1)}), bf16[8,128,1024]{2,1,0:T(8,128)(2,1)}, u32[]{:S(2)}, u32[]{:S(2)}) async-start(bf16[8,128,1024]{2,1,0:T(8,128)(2,1)} %finish.1), calls=%async_computation.3 | async-start | bytes 4194304 | tf_op jit(solution)/shard_map/all_to_all | solution.py:690
  535.6 1.3 collective-permute-start.6
  536.9 4.2 collective-permute-start.7
  541.1 14.6 %collective-permute-start.8 = (f32[12288]{0:T(1024)S(1)}, f32[12288]{0:T(1024)S(1)}, u32[]{:S(2)}, u32[]{:S(2)}) collective-permute-start(f32[12288]{0:T(1024)S(1)} %add.149), channel_id=1, source_target_pairs={{0,2},{2,0},{4,6},{6,4},{8,10},{10,8},{12,14},{14,12},{1,3},{3,1},... | collective-permute-start | bytes 147464 | tf_op jit(solution)/shard_map/ppermute | solution.py:863
  555.7 21.9 %collective-permute-start.9 = (f32[12288]{0:T(1024)S(1)}, f32[12288]{0:T(1024)S(1)}, u32[]{:S(2)}, u32[]{:S(2)}) collective-permute-start(f32[12288]{0:T(1024)S(1)} %add.150), channel_id=1, source_target_pairs={{0,4},{2,6},{4,0},{6,2},{8,12},{10,14},{12,8},{14,10},{1,5},{3,7},... | collective-permute-start | bytes 147464 | tf_op jit(solution)/shard_map/ppermute | solution.py:863
  577.6 14.2 %collective-permute-start.10 = (f32[12288]{0:T(1024)S(1)}, f32[12288]{0:T(1024)S(1)}, u32[]{:S(2)}, u32[]{:S(2)}) collective-permute-start(f32[12288]{0:T(1024)S(1)} %add.151), channel_id=1, source_target_pairs={{0,8},{2,10},{4,12},{6,14},{8,0},{10,2},{12,4},{14,6},{1,9},{3,11}... | collective-permute-start | bytes 147464 | tf_op jit(solution)/shard_map/ppermute | solution.py:863
  593.1 3.2 collective-permute-start.13
  612.1 2.0 collective-permute-start.12
  (15 other events, 315.0 us)
Sparse Core Ops, SparseCore 0:
  12.1 189.1 all-gather.5
  205.7 74.3 all-gather.3
  284.8 202.1 reduce-scatter.2
  519.9 90.5 reduce-scatter.4

commit v3 on v2

--- a/solution.py
+++ b/solution.py
@@ -1,5 +1,6 @@
 import jax
 import jax.numpy as jnp
+import numpy as np
 from jax import lax
 from jax.experimental import pallas as pl
 from jax.experimental.layout import Layout, with_layout_constraint
@@ -104,13 +105,27 @@
     return slice(side * wide, (side + 1) * wide)
 
 
-def qkv_kernel(one_ref, dy_ref, w_ref, bias_ref, cos_ref, sin_ref, after_ref, out_ref, grad_ref):
+def qkv_kernel(
+    one_ref, dy_ref, w_ref, bias_ref, cos_ref, sin_ref, lanes_ref, after_ref, out_ref, grad_ref
+):
     sides, groups, _, wide = w_ref.shape
     width = groups * HD
     lane = lax.broadcasted_iota(jnp.int32, (WIDE, PAIR), 1) % HD
     low_half = lane < ROT // 2
-    cosine = cos_ref[...]
-    sine_part = sin_ref[...]
+
+
+    def spread(table_ref, first):
+        table = jnp.concatenate([table_ref[i] for i in range(WIDE // TILE)], axis=1)
+        return lax.dot_general(
+            table,
+            lanes_ref[first : first + ROT // 2, :],
+            (((0,), (0,)), ((), ())),
+            precision=lax.Precision.HIGHEST,
+            preferred_element_type=F32,
+        )
+
+    cosine = spread(cos_ref, 0) + lanes_ref[ROT : ROT + 1, :]
+    sine_part = spread(sin_ref, ROT // 2)
 
     def product(rows_ref, part):
         return sum(
@@ -136,10 +151,11 @@
     grad_ref[...] = product(dy_ref, 3).astype(BF)
 
 
-def qkv_call(one, dy, w, bias, cosine, sine_part, after):
+def qkv_call(one, dy, w, bias, cosine, sine_part, lanes, after):
     tokens, feats = one.shape
     width = w.shape[1] * HD
     row = lambda size: pl.BlockSpec((WIDE, size), lambda i: (i, 0))
+    table = pl.BlockSpec((WIDE // TILE, ROT // 2, TILE), lambda i: (i, 0, 0))
     return pl.pallas_call(
         qkv_kernel,
         grid=(tokens // WIDE,),
@@ -148,8 +164,9 @@
             row(feats),
             pl.BlockSpec(w.shape, lambda i: (0, 0, 0, 0)),
             pl.BlockSpec((1, 3 * width), lambda i: (0, 0)),
-            row(PAIR),
-            row(PAIR),
+            table,
+            table,
+            pl.BlockSpec(lanes.shape, lambda i: (0, 0)),
             AFTER,
         ],
         out_specs=[row(3 * width), row(width)],
@@ -160,7 +177,7 @@
         compiler_params=params("arbitrary"),
         cost_estimate=cost(16 * tokens * feats * width, 8 * tokens * (feats + width)),
         name="qkv",
-    )(one, dy, w, bias, cosine, sine_part, after)
+    )(one, dy, w, bias, cosine, sine_part, lanes, after)
 
 
 def turn_back(g, cosine, sine_part):
@@ -424,30 +441,39 @@
     )(pre, two, act, dy)
 
 
-def head_grads_kernel(dq_ref, dk_ref, dv_ref, att_ref, one_ref, dy_ref, after_ref, out_ref):
-    groups, _, wide = out_ref.shape[1:]
+def head_grads_kernel(order_ref, dq_ref, dk_ref, dv_ref, att_ref, one_ref, dy_ref, *out_refs):
     pairs = ((dq_ref, one_ref), (dk_ref, one_ref), (dv_ref, one_ref), (att_ref, dy_ref))
-    for part, (left, right) in enumerate(pairs):
-        got = tn(left[...], right[...]).astype(BF)
-        out_ref[0, :, part * HD : (part + 1) * HD, :] = got.reshape(groups, HD, wide)
-
-
-def head_grads_call(dq, dk, dv, att, one, dy, sides, after):
+    for step, out_ref in enumerate(out_refs):
+        groups, _, wide = out_ref.shape
+
+        @pl.when(pl.program_id(0) == step)
+        def _():
+            for part, (left, right) in enumerate(pairs):
+                got = tn(left[...], right[...]).astype(BF)
+                out_ref[:, part * HD : (part + 1) * HD, :] = got.reshape(groups, HD, wide)
+
+
+def head_grads_call(order, dq, dk, dv, att, one, dy):
     tokens, feats = one.shape
     width = dq.shape[1]
+    sides = order.shape[0]
     groups, wide = width // HD, feats // sides
-    left = pl.BlockSpec((tokens, width), lambda f: (0, 0))
-    right = pl.BlockSpec((tokens, wide), lambda f: (0, f))
+    left = pl.BlockSpec((tokens, width), lambda i, *_: (0, 0))
+    right = pl.BlockSpec((tokens, wide), lambda i, order_ref: (0, order_ref[i]))
+    shape = (groups, 4 * HD, wide)
     return pl.pallas_call(
         head_grads_kernel,
-        grid=(sides,),
-        in_specs=[left] * 4 + [right] * 2 + [AFTER],
-        out_specs=pl.BlockSpec((1, groups, 4 * HD, wide), lambda f: (f, 0, 0, 0)),
-        out_shape=jax.ShapeDtypeStruct((sides, groups, 4 * HD, wide), BF),
+        grid_spec=pltpu.PrefetchScalarGridSpec(
+            num_scalar_prefetch=1,
+            grid=(sides,),
+            in_specs=[left] * 4 + [right] * 2,
+            out_specs=[pl.BlockSpec(shape, lambda i, *_: (0, 0, 0))] * sides,
+        ),
+        out_shape=[jax.ShapeDtypeStruct(shape, BF)] * sides,
         compiler_params=params("arbitrary"),
         cost_estimate=cost(12 * tokens * feats * width, 4 * tokens * (feats + 2 * width)),
         name="head_grads",
-    )(dq, dk, dv, att, one, dy, after)
+    )(order, dq, dk, dv, att, one, dy)
 
 
 def keep_and_send(core_ref, whole, keep_ref, send_ref, place):
@@ -466,7 +492,7 @@
     return [block, block], [jax.ShapeDtypeStruct(shape, F32), jax.ShapeDtypeStruct(shape, BF)]
 
 
-def output_kernel(core_ref, att_ref, act_ref, wd_ref, wout_ref, keep_ref, send_ref):
+def output_kernel(core_ref, att_ref, act_ref, wd_ref, wout_ref, after_ref, keep_ref, send_ref):
     sides, _, rows, wide = wout_ref.shape
     for f in range(sides):
         whole = nn(att_ref[...], block_of(wd_ref, f, 0, HD))
@@ -474,7 +500,7 @@
         keep_and_send(core_ref, whole, keep_ref, send_ref, columns(f, wide))
 
 
-def output_call(core, span, att, act, w_heads, w_units, rows):
+def output_call(core, span, att, act, w_heads, w_units, rows, after):
     tokens, width = att.shape
     units = act.shape[1]
     sides, groups, _, wide = w_units.shape
@@ -491,6 +517,7 @@
                 pl.BlockSpec((step, units), lambda i, *_: (i, 0)),
                 pl.BlockSpec((sides, groups, HD, wide), lambda i, *_: (0, 0, 3, 0)),
                 pl.BlockSpec((sides, groups, rows, wide), lambda i, *_: (0, 0, 1, 0)),
+                AFTER,
             ],
             out_specs=specs,
         ),
@@ -501,7 +528,7 @@
             2 * (tokens * (width + units + 2 * feats) + feats * (width + units)),
         ),
         name="output",
-    )(core, att, act, w_heads, w_units)
+    )(core, att, act, w_heads, w_units, after)
 
 
 def back_kernel(
@@ -588,30 +615,22 @@
     )(core, dq, dk, dv, pre, x, w_heads, w_units, gains, after)
 
 
-def fold_kernel(side_ref, own_ref, far_ref, after_ref, out_ref):
-    out_ref[...] = (own_ref[0].astype(F32) + far_ref[...].astype(F32)).astype(BF)
-
-
-def fold_call(side, full, far, after):
-    groups, rows, wide = far.shape
-    block = pl.BlockSpec((1, rows, wide), lambda i, *_: (i, 0, 0))
+def fold_kernel(own_ref, far_ref, after_ref, out_ref):
+    out_ref[...] = (own_ref[...].astype(F32) + far_ref[...].astype(F32)).astype(BF)
+
+
+def fold_call(own, far, after):
+    block = pl.BlockSpec((1,) + own.shape[1:], lambda i: (i, 0, 0))
     return pl.pallas_call(
         fold_kernel,
-        grid_spec=pltpu.PrefetchScalarGridSpec(
-            num_scalar_prefetch=1,
-            grid=(groups,),
-            in_specs=[
-                pl.BlockSpec((1, 1, rows, wide), lambda i, side_ref: (side_ref[0], i, 0, 0)),
-                block,
-                AFTER,
-            ],
-            out_specs=block,
-        ),
-        out_shape=jax.ShapeDtypeStruct(far.shape, BF),
+        grid=(own.shape[0],),
+        in_specs=[block, block, AFTER],
+        out_specs=block,
+        out_shape=jax.ShapeDtypeStruct(own.shape, BF),
         compiler_params=params("arbitrary"),
-        cost_estimate=cost(far.size * 2, far.size * 6),
+        cost_estimate=cost(own.size * 2, own.size * 6),
         name="fold",
-    )(side, full, far, after)
+    )(own, far, after)
 
 
 def finish_kernel(keep_ref, far_ref, x_ref, dy_ref, after_ref, out_ref):
@@ -799,15 +818,17 @@
     starts = lax.cummax(places * change, axis=0)
     begin = starts[::TILE] // TILE
     freqs = 10000.0 ** (-jnp.arange(0, ROT, 2, dtype=F32) / ROT)
-    relative = (places - starts).astype(F32)[:, None]
-    lane = jnp.arange(PAIR) % HD
+    angle = (places - starts).astype(F32).reshape(tiles, 1, TILE) * freqs[:, None]
+    cos_rows, sin_rows = jnp.cos(angle), jnp.sin(angle)
+    lane = np.arange(PAIR) % HD
+    spot = np.arange(ROT // 2)[:, None] == lane % (ROT // 2)
     turning = lane < ROT
-    lane_freqs = jnp.where(turning, freqs[lane % (ROT // 2)], 0.0)
-    angle = relative * lane_freqs
-    cos_lanes = jnp.cos(angle)
-    sin_lanes = jnp.sin(angle) * jnp.where(lane < ROT // 2, -1.0, 1.0)
-    cos_rows = cos_lanes[:, : ROT // 2].reshape(tiles, TILE, ROT // 2).transpose(0, 2, 1)
-    sin_rows = -sin_lanes[:, : ROT // 2].reshape(tiles, TILE, ROT // 2).transpose(0, 2, 1)
+    signs = np.where(lane < ROT // 2, -1.0, 1.0)
+    lanes = np.zeros((24, PAIR), np.float32)
+    lanes[: ROT // 2] = spot & turning
+    lanes[ROT // 2 : ROT] = (spot & turning) * signs
+    lanes[ROT] = ~turning
+    lanes = jnp.asarray(lanes)
 
     doc = starts.reshape(tiles, 1, TILE)
     x, one, two = merge_call(core_scalar, own_x, swap_cores(own_x), None, gains, shifts)
@@ -819,9 +840,15 @@
         grad_units = to_cores(unit_sums)
     else:
         grad_units = scatter_rows(unit_grads)
-    qkv, grad_att = qkv_call(one, dy, w_heads, qkv_shift, cos_lanes, sin_lanes, unit_grads)
+    qkv, grad_att = qkv_call(one, dy, w_heads, qkv_shift, cos_rows, sin_rows, lanes, unit_grads)
     attended, dq, dk, dv = attend_call(begin, qkv, grad_att, doc, cos_rows, sin_rows)
-    out_keep, out_send = output_call(core_scalar, span, attended, active, w_heads, w_units, unit_rows)
+    order = jnp.stack([1 - side, side]) if swap else jnp.zeros((1,), jnp.int32)
+    head_grads = head_grads_call(order, dq, dk, dv, attended, one, dy)
+    if swap:
+        far = side_swap(head_grads[0])
+    out_keep, out_send = output_call(
+        core_scalar, span, attended, active, w_heads, w_units, unit_rows, head_grads[0]
+    )
 
     bias_rows = out_biases.astype(F32)
     wide_x = own_x.astype(F32)
@@ -835,16 +862,14 @@
     out_low = (residual + out_part).astype(BF)
     hidden_out = from_chip(out_low)
 
-    head_grads = head_grads_call(dq, dk, dv, attended, one, dy, sides, out_low)
     e_keep, e_send, stats, qkv_sum = back_call(
-        core_scalar, span, dq, dk, dv, grad_pre, x, w_heads, w_units, gains, unit_rows, head_grads
+        core_scalar, span, dq, dk, dv, grad_pre, x, w_heads, w_units, gains, unit_rows, out_low
     )
     if swap:
-        far = lax.dynamic_index_in_dim(head_grads, 1 - side, 0, keepdims=False)
-        folded = fold_call(side.reshape(1), head_grads, side_swap(far), unit_sums)
+        folded = fold_call(head_grads[1], far, unit_sums)
         grad_heads = to_cores(sum_chips(folded, "tensor"))
     else:
-        grad_heads = scatter_rows(head_grads)
+        grad_heads = scatter_rows(head_grads[0][None])
     input_rows = finish_call(e_keep, swap_cores(e_send), own_x, upstream, hidden_out)
     input_grad = from_chip(input_rows)
 

time: 629 us -> 609 us (0.968)
  waiting for transfers between devices: 193 us -> 177 us
  other arithmetic: 23.3 us -> 15.2 us
    ppermute x2, waiting for transfers between devices: 32.3 us -> 19.1 us  [side_swap(): return lax.ppermute(v, 'fsdp', [(0, 1), (1, 0)])]
  transfers between devices with their start and end apart: 21 -> 21, of which waited for: 11 -> 12; matrix products, arithmetic and copies ran while one was open for 6% -> 4% of each run, Pallas kernels for 39% -> 41%
where the time goes in v3:
time: 609 us; the launch traced here: 603 us
  Pallas kernels  248 us (41%)
  waiting for transfers between devices  177 us (29%)
  blocking collectives  90.4 us (15%)
  starting transfers between devices  38.4 us (6%)
  local copies, waits for them, and re-layouts  19 us (3%)
  other arithmetic  15.2 us (2%)
  between operations  14.1 us (2%)
    all_to_all x1, waiting for transfers between devices, to_chip(): return lax.all_to_all(rows, 'tensor', 0, 0, tiled=True)  93.6 us
    all_to_all x1, blocking collectives, to_chip(): return lax.all_to_all(rows, 'tensor', 0, 0, tiled=True)  90.4 us
    pallas_call x1, Pallas kernels, attend_call(): pl.pallas_call(attend_kernel, grid_spec=pltpu.PrefetchScalarGridSpec(num_...  82 us
    ppermute x3, waiting for transfers between devices, body(): lax.ppermute(packed, 'tensor', [(i, i ^ bit) for i in range(chips)])  40.7 us
    pallas_call x1, Pallas kernels, units_call(): pl.pallas_call(units_kernel, grid=(units // step, tokens // WIDE), in_spe...  34.7 us
    pallas_call x1, Pallas kernels, back_call(): pl.pallas_call(back_kernel, grid_spec=pltpu.PrefetchScalarGridSpec(num_sc...  26.7 us
    pallas_call x1, Pallas kernels, unit_grads_call(): pl.pallas_call(unit_grads_kernel, grid=(sides, groups // taken), in_specs...  26 us
    all_to_all x2, starting transfers between devices, from_chip(): rows = lax.all_to_all(rows, 'tensor', 0, 0, tiled=True)  21.8 us
  transfers between devices with their start and end apart: 21, of which 12 were waited for; matrix products, arithmetic and copies ran while one was open for 4% of the time, Pallas kernels for 41%

profile of v3, /device:TPU:0, one launch (start us, length us, event | category | flops | bytes accessed | tf_op | source)
XLA Modules:
  0.0 603.0 jit_solution(6156015807016842000)
XLA Ops:
  12.0 90.4 %all_to_all.20.own_ref.x_ref = bf16[8,128,1024]{2,1,0:T(8,128)(2,1)S(1)} all-to-all(bf16[8,128,1024]{2,1,0:T(8,128)(2,1)} %param.13), channel_id=1, replica_groups=mesh['fsdp'=2,'tensor'=8,'ctx'=2] {'tensor'}, dimensions={0} | all-to-all | bytes 4194304 | tf_op jit(solution)/shard_map/all_to_all | solution.py:706
  102.5 4.5 all-to-all-start.1
  107.1 93.6 %all-to-all-done.1.own_ref.dy_ref = bf16[8,128,1024]{2,1,0:T(8,128)(2,1)} async-done(((bf16[8,128,1024]{2,1,0:T(8,128)(2,1)}), bf16[8,128,1024]{2,1,0:T(8,128)(2,1)}, u32[]{:S(2)}, u32[]{:S(2)}) %all-to-all-start.1) | async-done | bytes 2097184 | tf_op jit(solution)/shard_map/all_to_all | solution.py:706
  201.3 3.4 collective-permute-done.2
  206.8 9.1 %norms.1 = (bf16[2048,1024]{1,0:T(8,128)(2,1)}, bf16[2048,1024]{1,0:T(8,128)(2,1)}, bf16[2048,1024]{1,0:T(8,128)(2,1)}) custom-call(s32[1]{0:T(128)} %bitcast.2.core_ref, bf16[8,128,1024]{2,1,0:T(8,128)(2,1)} %copy-done.2, bf16[8,128,1024]{2,1,0:T(8,128)(2,1)} %collective-permute-done.far_ref, f32[2,1024]{1,0:T(2,128)} %convert_element_type.47.gain_ref, ...), custom_call_target="tpu_custom_call" | custom-call | flops 25165824 | bytes 16777216 | tf_op jit(solution)/shard_map/norms/pallas_call | solution.py:84
  216.0 6.6 %merge.1.dy_ref = bf16[2048,1024]{1,0:T(8,128)(2,1)} custom-call(s32[1]{0:T(128)} %bitcast.2.core_ref, bf16[8,128,1024]{2,1,0:T(8,128)(2,1)} %all-to-all-done.1.own_ref.dy_ref, bf16[8,128,1024]{2,1,0:T(8,128)(2,1)} %collective-permute-done.1.far_ref, bf16[2048,1024]{1,0:T(8,128)(2,1)} %get-tuple-element.31.after_ref.one_ref), custom_call_target="tpu_custom_call" | custom-call | flops 25165824 | bytes 8388608 | tf_op jit(solution)/shard_map/merge/pallas_call | solution.py:84
  224.1 34.7 %units.1 = (bf16[2048,2048]{1,0:T(8,128)(2,1)}, bf16[2048,2048]{1,0:T(8,128)(2,1)}, f32[1,2048]{1,0:T(1,128)}) custom-call(bf16[2048,1024]{1,0:T(8,128)(2,1)} %get-tuple-element.32.two_ref, bf16[2048,1024]{1,0:T(8,128)(2,1)} %merge.1.dy_ref, bf16[2,8,528,512]{3,2,1,0:T(8,128)(2,1)} %bitcast.110, bf16[2,8,528,512]{3,2,1,0:T(8,128)(2,1)} %bitcast.111, ...), custom_call_target="tpu_custom_call" | custom-call | flops 42949672960 | bytes 83886080 | tf_op jit(solution)/shard_map/units/pallas_call | solution.py:394
  258.8 26.0 %unit_grads.1.after_ref = bf16[2,8,512,512]{3,2,1,0:T(8,128)(2,1)} custom-call(bf16[2048,2048]{1,0:T(8,128)(2,1)} %get-tuple-element.33.pre_ref, bf16[2048,1024]{1,0:T(8,128)(2,1)} %get-tuple-element.32.two_ref, bf16[2048,2048]{1,0:T(8,128)(2,1)} %get-tuple-element.34.act_ref, bf16[2048,1024]{1,0:T(8,128)(2,1)} %merge.1.dy_ref), custom_call_target="tpu_custom_call" | custom-call | flops 25769803776 | bytes 41943040 | tf_op jit(solution)/shard_map/unit_grads/pallas_call | solution.py:432
  290.3 15.5 %qkv.1 = (bf16[2048,1536]{1,0:T(8,128)(2,1)}, bf16[2048,512]{1,0:T(8,128)(2,1)}) custom-call(bf16[2048,1024]{1,0:T(8,128)(2,1)} %get-tuple-element.31.after_ref.one_ref, bf16[2048,1024]{1,0:T(8,128)(2,1)} %merge.1.dy_ref, bf16[2,8,256,512]{3,2,1,0:T(8,128)(2,1)} %bitcast.114, f32[1,1536]{1,0:T(1,128)} %reshape.258.bias_ref, ...), custom_call_target="tpu_custom_call" | custom-call | flops 17179869184 | bytes 25165824 | tf_op jit(solution)/shard_map/qkv/pallas_call | solution.py:159
  305.8 82.0 %attend.1 = (bf16[2048,512]{1,0:T(8,128)(2,1)}, bf16[2048,512]{1,0:T(8,128)(2,1)}, bf16[2048,512]{1,0:T(8,128)(2,1)}, bf16[2048,512]{1,0:T(8,128)(2,1)}) custom-call(s32[8]{0:T(128)} %and_select_fusion.begin_ref, bf16[2048,1536]{1,0:T(8,128)(2,1)} %get-tuple-element.35.q_ref.k_ref.v_ref, bf16[2048,1536]{1,0:T(8,128)(2,1)} %get-tuple-element.35.q_ref.k_ref.v_ref, ...), custom_call_target="tpu_custom_call" | custom-call | flops 40265318400 | bytes 16777216 | tf_op jit(solution)/shard_map/attend/pallas_call | solution.py:324
  387.9 16.7 %head_grads.1 = (bf16[8,256,512]{2,1,0:T(8,128)(2,1)}, bf16[8,256,512]{2,1,0:T(8,128)(2,1)}) custom-call(s32[2]{0:T(128)} %pad_add_fusion.order_ref, bf16[2048,512]{1,0:T(8,128)(2,1)} %get-tuple-element.38.dq_ref, bf16[2048,512]{1,0:T(8,128)(2,1)} %get-tuple-element.39.dk_ref, bf16[2048,512]{1,0:T(8,128)(2,1)} %get-tuple-element.40.dv_ref, ...), custom_call_target="tpu_custom_call" | custom-call | flops 12884901888 | bytes 16777216 | tf_op jit(solution)/shard_map/head_grads/pallas_call | solution.py:464
  404.6 16.2 %output.1 = (f32[8,128,1024]{2,1,0:T(8,128)}, bf16[8,128,1024]{2,1,0:T(8,128)(2,1)}) custom-call(s32[1]{0:T(128)} %bitcast.2.core_ref, bf16[2048,512]{1,0:T(8,128)(2,1)} %get-tuple-element.37.att_ref, bf16[2048,2048]{1,0:T(8,128)(2,1)} %get-tuple-element.34.act_ref, bf16[2,8,256,512]{3,2,1,0:T(8,128)(2,1)} %bitcast.115, bf16[2,8,528,512]{3,2,1,0:T(8,128)(2,1)} %bitcast.112, ...), custom_call_target="tpu_custom_call" | custom-call | flops 16106127360 | bytes 24117248 | tf_op jit(solution)/shard_map/output/pallas_call | solution.py:510
  425.2 4.9 add_convert_fusion.after_ref
  430.1 16.0 %all-to-all-start.2 = ((bf16[8,128,1024]{2,1,0:T(8,128)(2,1)}), bf16[8,128,1024]{2,1,0:T(8,128)(2,1)S(1)}, u32[]{:S(2)}, u32[]{:S(2)}) async-start(bf16[8,128,1024]{2,1,0:T(8,128)(2,1)} %add_convert_fusion.after_ref), calls=%async_computation.2 | async-start | bytes 4194304 | tf_op jit(solution)/shard_map/all_to_all | solution.py:709
  446.1 26.7 %back.1 = (f32[8,128,1024]{2,1,0:T(8,128)}, bf16[8,128,1024]{2,1,0:T(8,128)(2,1)}, f32[4,1024]{1,0:T(4,128)}, f32[1,1536]{1,0:T(1,128)}) custom-call(s32[1]{0:T(128)} %bitcast.2.core_ref, bf16[2048,512]{1,0:T(8,128)(2,1)} %get-tuple-element.38.dq_ref, bf16[2048,512]{1,0:T(8,128)(2,1)} %get-tuple-element.39.dk_ref, ...), custom_call_target="tpu_custom_call" | custom-call | flops 22548578304 | bytes 34603008 | tf_op jit(solution)/shard_map/back/pallas_call | solution.py:582
  472.9 16.1 %collective-permute-done.11.far_ref = bf16[8,256,512]{2,1,0:T(8,128)(2,1)} collective-permute-done((bf16[8,256,512]{2,1,0:T(8,128)(2,1)}, bf16[8,256,512]{2,1,0:T(8,128)(2,1)}, u32[]{:S(2)}, u32[]{:S(2)}) %collective-permute-start.11) | collective-permute-done | bytes 2097184 | tf_op jit(solution)/shard_map/ppermute | solution.py:739
  488.9 6.2 %fold.1 = bf16[8,256,512]{2,1,0:T(8,128)(2,1)} custom-call(bf16[8,256,512]{2,1,0:T(8,128)(2,1)} %get-tuple-element.50.own_ref, bf16[8,256,512]{2,1,0:T(8,128)(2,1)} %collective-permute-done.11.far_ref, bf16[1,512,512]{2,1,0:T(8,128)(2,1)} %reduce-scatter.3.cloned.1.call-done.after_ref), custom_call_target="tpu_custom_call" | custom-call | flops 2097152 | bytes 6291456 | tf_op jit(solution)/shard_map/fold/pallas_call | solution.py:624
  498.9 8.7 %finish.1 = bf16[8,128,1024]{2,1,0:T(8,128)(2,1)} custom-call(f32[8,128,1024]{2,1,0:T(8,128)} %get-tuple-element.45.keep_ref, bf16[8,128,1024]{2,1,0:T(8,128)(2,1)} %collective-permute-done.5.far_ref, bf16[8,128,1024]{2,1,0:T(8,128)(2,1)} %copy-done.2, bf16[8,128,1024]{2,1,0:T(8,128)(2,1)} %all-to-all-done.1.own_ref.dy_ref, bf16[8,128,1024]{2,1,0:T(8,128)(2,1)} %copy-done.4), custom_call_target="tpu_custom_call" | custom-call | flops 20971520 | bytes 12582912 | tf_op jit(solution)/shard_map/finish/pallas_call | solution.py:649
  507.5 5.9 all-to-all-start.3
  522.6 11.9 %collective-permute-done.8 = f32[12288]{0:T(1024)S(1)} collective-permute-done((f32[12288]{0:T(1024)S(1)}, f32[12288]{0:T(1024)S(1)}, u32[]{:S(2)}, u32[]{:S(2)}) %collective-permute-start.8) | collective-permute-done | bytes 49184 | tf_op jit(solution)/shard_map/ppermute | solution.py:888
  536.0 17.8 %collective-permute-done.9 = f32[12288]{0:T(1024)S(1)} collective-permute-done((f32[12288]{0:T(1024)S(1)}, f32[12288]{0:T(1024)S(1)}, u32[]{:S(2)}, u32[]{:S(2)}) %collective-permute-start.9) | collective-permute-done | bytes 49184 | tf_op jit(solution)/shard_map/ppermute | solution.py:888
  553.8 3.3 collective-permute-start.10
  557.2 11.0 %collective-permute-done.10 = f32[12288]{0:T(1024)S(1)} collective-permute-done((f32[12288]{0:T(1024)S(1)}, f32[12288]{0:T(1024)S(1)}, u32[]{:S(2)}, u32[]{:S(2)}) %collective-permute-start.10) | collective-permute-done | bytes 49184 | tf_op jit(solution)/shard_map/ppermute | solution.py:888
  572.8 14.2 %reduce-scatter.5.cloned.1.call-done = bf16[1,256,512]{2,1,0:T(8,128)(2,1)} async-done(((bf16[8,256,512]{2,1,0:T(8,128)(2,1)}), bf16[1,256,512]{2,1,0:T(8,128)(2,1)}) %reduce-scatter.5.cloned.1.call-update) | async-done | bytes 262160 | tf_op jit(solution)/shard_map/reduce_scatter | solution.py:742
  (151 shorter events, 47.5 us)
Async XLA Ops:
  7.2 215.4 %all-gather.6.cloned.1.call-start = ((), (), s32[]{:S(2)}) async-start(), calls=%async_computation.9 | async-start | bytes 9191424 | tf_op jit(solution)/shard_map/all_gather | solution.py:730
  9.3 1.7 collective-permute-start.3
  102.5 98.3 %copy-start.9 = (bf16[2,64,256]{2,1,0:T(8,128)(2,1)S(1)}, bf16[2,64,256]{2,1,0:T(8,128)(2,1)}, u32[]{:S(2)}) copy-start(bf16[2,64,256]{2,1,0:T(8,128)(2,1)} %param.19) | copy-start | bytes 196612
  102.5 103.1 %copy-start.14 = (bf16[2,1024]{1,0:T(2,128)(2,1)S(1)}, bf16[2,1024]{1,0:T(2,128)(2,1)}, u32[]{:S(2)}) copy-start(bf16[2,1024]{1,0:T(2,128)(2,1)} %param.15) | copy-start | bytes 12292
  102.5 103.8 %copy-start.15 = (bf16[2,1024]{1,0:T(2,128)(2,1)S(1)}, bf16[2,1024]{1,0:T(2,128)(2,1)}, u32[]{:S(2)}) copy-start(bf16[2,1024]{1,0:T(2,128)(2,1)} %param.16) | copy-start | bytes 12292
  102.5 98.3 %all-to-all-start.1 = ((bf16[8,128,1024]{2,1,0:T(8,128)(2,1)}), bf16[8,128,1024]{2,1,0:T(8,128)(2,1)}, u32[]{:S(2)}, u32[]{:S(2)}) async-start(bf16[8,128,1024]{2,1,0:T(8,128)(2,1)} %param.24), calls=%async_computation.1 | async-start | bytes 4194304 | tf_op jit(solution)/shard_map/all_to_all | solution.py:706
  107.0 183.3 %all-gather.4.cloned.1.call-start = ((), (), s32[]{:S(2)}) async-start(), calls=%async_computation.6 | async-start | bytes 4456448 | tf_op jit(solution)/shard_map/all_gather | solution.py:730
  107.0 99.8 %collective-permute-start = (bf16[8,128,1024]{2,1,0:T(8,128)(2,1)S(1)}, bf16[8,128,1024]{2,1,0:T(8,128)(2,1)}, u32[]{:S(2)}, u32[]{:S(2)}) collective-permute-start(bf16[8,128,1024]{2,1,0:T(8,128)(2,1)S(1)} %all_to_all.20.own_ref.x_ref), channel_id=1, source_target_pairs={{0,1},{1,0},{2,3},{3,2},{4,5},{5,4},{6,7},{7,6},{8,9},{9,8},{10,11... | collective-permute-start | bytes 6291464 | tf_op jit(solution)/shard_map/ppermute | solution.py:662
  200.7 15.2 %collective-permute-start.1 = (bf16[8,128,1024]{2,1,0:T(8,128)(2,1)}, bf16[8,128,1024]{2,1,0:T(8,128)(2,1)}, u32[]{:S(2)}, u32[]{:S(2)}) collective-permute-start(bf16[8,128,1024]{2,1,0:T(8,128)(2,1)} %all-to-all-done.1.own_ref.dy_ref), channel_id=1, source_target_pairs={{0,1},{1,0},{2,3},{3,2},{4,5},{5,4},{6,7},{7,6},{8,9},{9,8},{10,11... | collective-permute-start | bytes 6291464 | tf_op jit(solution)/shard_map/ppermute | solution.py:662
  200.8 3.9 collective-permute-start.2
  205.6 283.4 %reduce-scatter.3.cloned.1.call-start = ((), (), s32[]{:S(2)}) async-start(), calls=%async_computation.7 | async-start | bytes 8912896 | tf_op jit(solution)/shard_map/reduce_scatter | solution.py:742
  420.8 4.4 collective-permute-start.4
  421.2 67.7 %collective-permute-start.11 = (bf16[8,256,512]{2,1,0:T(8,128)(2,1)}, bf16[8,256,512]{2,1,0:T(8,128)(2,1)}, u32[]{:S(2)}, u32[]{:S(2)}) collective-permute-start(bf16[8,256,512]{2,1,0:T(8,128)(2,1)} %get-tuple-element.41.after_ref), channel_id=1, source_target_pairs={{0,16},{16,0},{1,17},{17,1},{2,18},{18,2},{3,19},{19,3},{4,20},{20... | collective-permute-start | bytes 6291464 | tf_op jit(solution)/shard_map/ppermute | solution.py:739
  430.1 67.5 %all-to-all-start.2 = ((bf16[8,128,1024]{2,1,0:T(8,128)(2,1)}), bf16[8,128,1024]{2,1,0:T(8,128)(2,1)S(1)}, u32[]{:S(2)}, u32[]{:S(2)}) async-start(bf16[8,128,1024]{2,1,0:T(8,128)(2,1)} %add_convert_fusion.after_ref), calls=%async_computation.2 | async-start | bytes 4194304 | tf_op jit(solution)/shard_map/all_to_all | solution.py:709
  446.1 140.9 %reduce-scatter.5.cloned.1.call-start = ((), (), s32[]{:S(2)}) async-start(), calls=%async_computation.8 | async-start | bytes 2359296 | tf_op jit(solution)/shard_map/reduce_scatter | solution.py:742
  472.8 22.3 %collective-permute-start.5 = (bf16[8,128,1024]{2,1,0:T(8,128)(2,1)}, bf16[8,128,1024]{2,1,0:T(8,128)(2,1)}, u32[]{:S(2)}, u32[]{:S(2)}) collective-permute-start(bf16[8,128,1024]{2,1,0:T(8,128)(2,1)} %get-tuple-element.46), channel_id=1, source_target_pairs={{0,1},{1,0},{2,3},{3,2},{4,5},{5,4},{6,7},{7,6},{8,9},{9,8},{10,11... | collective-permute-start | bytes 6291464 | tf_op jit(solution)/shard_map/ppermute | solution.py:662
  507.5 65.1 %all-to-all-start.3 = ((bf16[8,128,1024]{2,1,0:T(8,128)(2,1)}), bf16[8,128,1024]{2,1,0:T(8,128)(2,1)}, u32[]{:S(2)}, u32[]{:S(2)}) async-start(bf16[8,128,1024]{2,1,0:T(8,128)(2,1)} %finish.1), calls=%async_computation.3 | async-start | bytes 4194304 | tf_op jit(solution)/shard_map/all_to_all | solution.py:709
  514.5 1.3 collective-permute-start.6
  515.9 4.2 collective-permute-start.7
  520.0 14.5 %collective-permute-start.8 = (f32[12288]{0:T(1024)S(1)}, f32[12288]{0:T(1024)S(1)}, u32[]{:S(2)}, u32[]{:S(2)}) collective-permute-start(f32[12288]{0:T(1024)S(1)} %add.100), channel_id=1, source_target_pairs={{0,2},{2,0},{4,6},{6,4},{8,10},{10,8},{12,14},{14,12},{1,3},{3,1},... | collective-permute-start | bytes 147464 | tf_op jit(solution)/shard_map/ppermute | solution.py:888
  534.5 19.3 %collective-permute-start.9 = (f32[12288]{0:T(1024)S(1)}, f32[12288]{0:T(1024)S(1)}, u32[]{:S(2)}, u32[]{:S(2)}) collective-permute-start(f32[12288]{0:T(1024)S(1)} %add.101), channel_id=1, source_target_pairs={{0,4},{2,6},{4,0},{6,2},{8,12},{10,14},{12,8},{14,10},{1,5},{3,7},... | collective-permute-start | bytes 147464 | tf_op jit(solution)/shard_map/ppermute | solution.py:888
  553.8 14.3 %collective-permute-start.10 = (f32[12288]{0:T(1024)S(1)}, f32[12288]{0:T(1024)S(1)}, u32[]{:S(2)}, u32[]{:S(2)}) collective-permute-start(f32[12288]{0:T(1024)S(1)} %add.102), channel_id=1, source_target_pairs={{0,8},{2,10},{4,12},{6,14},{8,0},{10,2},{12,4},{14,6},{1,9},{3,11}... | collective-permute-start | bytes 147464 | tf_op jit(solution)/shard_map/ppermute | solution.py:888
  569.5 3.2 collective-permute-start.13
  588.6 2.0 collective-permute-start.12
  (13 other events, 308.7 us)
Sparse Core Ops, SparseCore 0:
  12.1 189.1 all-gather.5
  205.7 74.3 all-gather.3
  284.9 194.1 reduce-scatter.2
  495.2 91.6 reduce-scatter.4
